TPU v7x, 256 devices: a whole 4x4x8 slice. The times are simulated.
256 devices in a mesh: coarse: 16 (over z, core), fine: 16 (over y, x).
Axes of the slice: x: 4, y: 4, z: 8, core: 2. Of those that a mesh axis runs over, the one named last changes fastest.
Arguments:
- source_term: float32 [256, 256, 256], P('coarse', 'fine'), may hold values from -4 to 10
- conduct_x: float32 [256, 256, 256], P('coarse', 'fine'), may hold values from 0.5 to 4
- conduct_y: float32 [256, 256, 256], P('coarse', 'fine'), may hold values from 0.5 to 4
- conduct_z: float32 [256, 256, 256], P('coarse', 'fine'), may hold values from 0.5 to 4
- absorption: float32 [256, 256, 256], P('coarse', 'fine'), may hold values from 0.05 to 1
- block_active: int32 [16, 16, 16], P('coarse', 'fine'), may hold values 0 or 1
Outputs:
- solution_field: float32 [256, 256, 256], P('coarse', 'fine')
- coarse_correction: float32 [64, 64, 64], P('coarse', 'fine')
All inputs are finite; a program needn't handle non-finite values. No bound on the sum of `block_active` on one device may be relied on, other than what follows from the above.
Results may differ from a plain program's by a relative error of at most 0.0003.
Values sent between devices are 32-bit elements; how exact they have to be, the bound alone decides.
No kernel may reach another device: no remote copies, remote signals or barrier semaphores. Data moves between devices by JAX's collectives and lax.ppermute only.
A program may use at most 64 MiB of HBM per device.

v0:
```python
import jax
import jax.numpy as jnp
from jax import lax
from jax.experimental import pallas as pl
from jax.experimental.pallas import tpu as pltpu
from jax.sharding import PartitionSpec as P

f32 = jnp.float32
bf16 = jnp.bfloat16
fine_low = 0.25
fine_high = 2.0
coarse_share = 0.125
SIDE = 16
LONG = 256
ROWS = SIDE + 6
RING = 24
VMEM = pl.BlockSpec(memory_space=pltpu.VMEM)
SMEM = pl.BlockSpec(memory_space=pltpu.SMEM)
LIMIT = 24 * 1024 * 1024


def factors(lower, upper):
    center = 0.5 * (upper + lower)
    radius = 0.5 * (upper - lower)
    aspect = center / radius
    p0 = 1.0 / aspect
    p1 = 1.0 / (2.0 * aspect - p0)
    p2 = 1.0 / (2.0 * aspect - p1)
    return center, p1 * p0, 2.0 * p1 / radius, p2 * p1, 2.0 * p2 / radius


FINE = factors(fine_low, fine_high)


def iota(shape, axis):
    return lax.broadcasted_iota(jnp.int32, shape, axis)


def back(values, axis):
    return pltpu.roll(values, 1, axis)


def ahead(values, axis):
    return pltpu.roll(values, values.shape[axis] - 1, axis)


def call(kernel, outs, scratch=(), ins=None):
    return pl.pallas_call(
        kernel,
        out_shape=[jax.ShapeDtypeStruct(s, f32) for s in outs],
        in_specs=ins,
        out_specs=[VMEM] * len(outs),
        scratch_shapes=list(scratch),
        compiler_params=pltpu.CompilerParams(vmem_limit_bytes=LIMIT),
    )


def pack_first(*refs):
    fields, pair, sems = refs[:5], refs[5:7], refs[7]
    even = lax.axis_index("coarse") % 2 == 0

    def fill(up, down):
        copies = []
        for n, field in enumerate(fields):
            first = 12 if n == 1 else 13
            at = UP_AT[n] + first - 13
            copies.append((field.at[first:16], up.at[at : at + 16 - first]))
            copies.append((field.at[0:3], down.at[3 * n : 3 * n + 3]))
        copies = [pltpu.make_async_copy(a, b, sems.at[k]) for k, (a, b) in enumerate(copies)]
        for copy in copies:
            copy.start()
        for copy in copies:
            copy.wait()

    @pl.when(even)
    def _():
        fill(*pair)

    @pl.when(jnp.logical_not(even))
    def _():
        fill(*pair[::-1])


def pack_first_call(fields):
    return pl.pallas_call(
        pack_first,
        out_shape=[jax.ShapeDtypeStruct((16, SIDE, LONG), f32)] * 2,
        in_specs=[pl.BlockSpec(memory_space=pltpu.HBM)] * 5,
        out_specs=[VMEM] * 2,
        scratch_shapes=[pltpu.SemaphoreType.DMA((10,))],
    )(*fields)


UP_AT = (0, 4, 7, 10, 13)


def sum_lanes(last_only):
    cell, lane = iota((LONG, 128), 0), iota((LONG, 128), 1)
    hit = cell // 4 == lane
    if last_only:
        hit = hit & (cell % 4 == 3)
    return hit.astype(bf16)


def sum_rows(last_only):
    block, cell = iota((8, SIDE), 0), iota((8, SIDE), 1)
    hit = cell // 4 == block
    if last_only:
        hit = hit & (cell % 4 == 3)
    return hit.astype(bf16)


def parts_of(values):
    first = values.astype(bf16)
    rest = values - first.astype(f32)
    second = rest.astype(bf16)
    return first, second, (rest - second.astype(f32)).astype(bf16)


def by_right(values, choose):
    return sum(jnp.dot(p, choose, preferred_element_type=f32) for p in parts_of(values))


def by_left(choose, values):
    return sum(jnp.dot(choose, p, preferred_element_type=f32) for p in parts_of(values))


def coarsen(cx, cy, cz, ab, active, out, mask):
    lanes, last = sum_lanes(False), sum_lanes(True)
    rows, lastrow = sum_rows(False), sum_rows(True)

    def coarse(n, part, left, right):
        total = by_right(jnp.concatenate([part(4 * a) for a in range(4)], axis=0), right)
        for a in range(4):
            out[n, a] = by_left(left, total[SIDE * a : SIDE * a + SIDE])

    def layers(ref):
        return lambda x: (ref[x] + ref[x + 1]) + (ref[x + 2] + ref[x + 3])

    coarse(0, lambda x: cx[x + 3], rows, lanes)
    coarse(1, layers(cy), lastrow, lanes)
    coarse(2, layers(cz), rows, last)
    coarse(3, layers(ab), rows, lanes)
    spread = ((iota((16, 128), 1) // 4) == iota((16, 128), 0)).astype(bf16)
    line = jnp.broadcast_to(active[0].astype(f32), (8, 16)).astype(bf16)
    mask[...] = jnp.dot(line, spread, preferred_element_type=f32)


def diagonal(cx_i, cxl_i, cy_i, cz_i, ab_i):
    row, lane = iota((SIDE, LONG), 0), iota((SIDE, LONG), 1)
    g = cx_i + cxl_i + cy_i + cz_i + ab_i
    g = g + jnp.where(row == 0, 0.0, back(cy_i, 0))
    return g + jnp.where(lane == 0, 0.0, back(cz_i, 1))


def strips(src_i, cx_i, cy_i, cz_i, g, inside, beyond=None):
    start = jnp.where(inside, src_i / (FINE[0] * g), 0.0)
    pieces = (src_i, cx_i, cy_i, cz_i, g)
    third = cy_i[13:14] if beyond is None else beyond[15:16]
    top = jnp.concatenate([p[14:16] for p in pieces] + [start[13:14], third], axis=0)
    bottom = jnp.concatenate([p[0:2] for p in pieces] + [start[2:3], start[2:3]], axis=0)
    return top, bottom


def pack_inner(flags, src, cx, cy, cz, ab, diag, first, second):
    even = flags[4] > 0
    for x in range(1, SIDE):
        g = diagonal(cx[x], cx[x - 1], cy[x], cz[x], ab[x])
        diag[x] = g
        top, bottom = strips(src[x], cx[x], cy[x], cz[x], g, True)
        at = (x - 1) % 8, pl.ds(12 * ((x - 1) // 8), 12)
        first[at] = jnp.where(even, top, bottom)
        second[at] = jnp.where(even, bottom, top)


def pack_outer(flags, src, cx, cy, cz, ab, one, two, diag, first, second):
    even = flags[4] > 0
    has_low, has_high = flags[0] > 0, flags[1] > 0
    low, high = sides(one, two, flags[5] > 0, has_low, has_high)
    layers = []
    for k in range(3):
        f = [low(UP_AT[n] + k) for n in range(5)]
        layers.append((f, low(3 + k), has_low, low(UP_AT[2]) if k == 1 else None))
    layers.append(([ref[0] for ref in (src, cx, cy, cz, ab)], low(6), True, None))
    for k in range(3):
        f = [high(3 * n + k) for n in range(5)]
        before = cx[15] if k == 0 else high(3 + k - 1)
        layers.append((f, before, has_high, high(8) if k == 1 else None))
    for k, (f, before, inside, beyond) in enumerate(layers):
        g = diagonal(f[1], before, *f[2:])
        diag[k] = g
        if 1 <= k < 6:
            top, bottom = strips(*f[:4], g, inside, beyond)
            at = (k - 1) % 3, pl.ds(12 * ((k - 1) // 3), 12)
            first[at] = jnp.where(even, top, bottom)
            second[at] = jnp.where(even, bottom, top)


def sides(one, two, even, has_low, has_high):
    keep_low, keep_high = has_low.astype(f32), has_high.astype(f32)

    def low(*at):
        return jnp.where(even, two[at], one[at]) * keep_low

    def high(*at):
        return jnp.where(even, one[at], two[at]) * keep_high

    return low, high


def near(i, u, cx, cy, cz):
    here = u[i]
    cy_i, cz_i = cy[i], cz[i]
    total = cx[i] * u[i + 1] + cx[i - 1] * u[i - 1]
    total = total + (cy_i * ahead(here, 0) + back(cy_i * here, 0))
    return total + (cz_i * ahead(here, 1) + back(cz_i * here, 1))


def join(layers):
    total = layers[0]
    for k, v in enumerate(layers[1:], 1):
        v = pltpu.roll(v, 64, 1) if k >= 2 else v
        total = total + (pltpu.roll(v, 4, 0) if k % 2 else v)
    return total


class Layers:
    def __init__(self, inner, outer=None):
        self.inner, self.outer = inner, outer

    def __getitem__(self, i):
        if 4 <= i < 19:
            return self.inner[i - 4]
        return self.outer[i if i < 4 else i - 15]

    def __setitem__(self, i, value):
        self.inner[i - 4] = value


class Over(dict):
    def __init__(self, inner, rows=None):
        self.inner, self.rows = inner, rows

    def __missing__(self, i):
        return self.inner[i - 4 if self.rows is None else self.rows[i]]


def own_layer(x, inner, outer, first, last, skip):
    return inner[x - first] if first <= x <= last else outer[x if x < first else x - skip]


def ring_layer(fields, g, lo, hi, hit, face=None):
    src_i, cx_i, cy_i, cz_i = fields
    row, lane = iota((RING, LONG), 0), iota((RING, LONG), 1)
    none1, none4 = jnp.zeros((1, LONG), f32), jnp.zeros((4, LONG), f32)

    def ring(own, n):
        return jnp.concatenate([own, hi[2 * n : 2 * n + 2], none4, lo[2 * n : 2 * n + 2]], axis=0)

    src_r, cx_r, cz_r, g = ring(src_i, 0), ring(cx_i, 1), ring(cz_i, 3), ring(g, 4)
    cy_r = jnp.concatenate([cy_i, hi[4:6], none1, none1, none1, lo[11:12], lo[4:6]], axis=0)
    if face is not None:
        cy_r = jnp.where(row == 23, face, cy_r)
    g = g + jnp.where((row == 0) | (row == 16), back(cy_r, 0), 0.0)
    inv = jnp.where(hit, 1.0 / g, 0.0)
    u = src_r * inv * (1.0 / FINE[0])
    u = jnp.where(row == 18, hi[10:11], u)
    u = jnp.where(row == 21, lo[10:11], u)
    return cx_r, cy_r, jnp.where(lane == LONG - 1, 0.0, cz_r), g, inv, src_r, u


def inside_ring(flags):
    row = iota((RING, LONG), 0)
    return (row < 16) | ((row < 18) & (flags[3] > 0)) | ((row >= 22) & (flags[2] > 0))


EDGE_ROWS = ((4, 5, 6, 16, 17, 18), (4, 5, 17, 18), (5, 6, 16, 17), (6, 7, 15, 16))
EDGES = [{i: k + sum(map(len, EDGE_ROWS[:n])) for k, i in enumerate(v)} for n, v in enumerate(EDGE_ROWS)]


def smooth_inner(
    flags, src, cx, cy, cz, diag, one, two,
    cx_o, cy_o, cz_o, g_o, inv_o, edge, iterate, resid, u0, u1, u2, r,
):
    center, m1, q1, m2, q2 = FINE
    left, right = sides(one, two, flags[4] > 0, flags[2] > 0, flags[3] > 0)
    hit = inside_ring(flags)
    made = [Layers(ref) for ref in (cx_o, cy_o, cz_o, g_o, inv_o, r, u0)]
    u1, u2 = Layers(u1), Layers(u2)
    for i in range(4, 19):
        x, at = i - 3, ((i - 4) % 8, pl.ds(12 * ((i - 4) // 8), 12))
        fields = src[x], cx[x], cy[x], cz[x]
        for out, value in zip(made, ring_layer(fields, diag[x], left(*at), right(*at), hit)):
            out[i] = value
    cx, cy, cz, g, inv, r, u0 = made
    for i in range(5, 18):
        u = u0[i]
        v = r[i] - (g[i] * u - near(i, u0, cx, cy, cz))
        r[i] = v
        u1[i] = m1 * u + q1 * (inv[i] * v)
    for i in range(6, 17):
        u = u1[i]
        v = r[i] - (g[i] * u - near(i, u1, cx, cy, cz))
        r[i] = v
        v = m2 * u + q2 * (inv[i] * v)
        u2[i] = v
        iterate[i - 6] = (u0[i] + u + v)[:SIDE]
    for values, rows in zip((r, u0, u1, u2), EDGES):
        for i, at in rows.items():
            edge[at] = values[i]
    for i in range(7, 16):
        resid[i - 7] = (r[i] - (g[i] * u2[i] - near(i, u2, cx, cy, cz)))[:SIDE]


def smooth_outer(
    flags, src, cx, cy, cz, one_x, two_x, diag, one, two, coarse, active,
    cx_i, cy_i, cz_i, g_i, inv_i, edge, resid_i,
    cx_o, cy_o, cz_o, g_o, inv_o, iterate, resid, packed, weight, first, second,
):
    center, m1, q1, m2, q2 = FINE
    has_low, has_high = flags[0] > 0, flags[1] > 0
    low, high = sides(one_x, two_x, flags[5] > 0, has_low, has_high)
    left, right = sides(one, two, flags[4] > 0, flags[2] > 0, flags[3] > 0)
    hit = inside_ring(flags)
    own_row = iota((RING, LONG), 0) < SIDE
    none12 = jnp.zeros((12, LONG), f32)
    layers = [([low(UP_AT[n] + k) for n in range(4)], has_low) for k in range(3)]
    layers.append(([ref[0] for ref in (src, cx, cy, cz)], True))
    layers += [([high(3 * n + k) for n in range(4)], has_high) for k in range(3)]
    made = [Over(ref) for ref in (cx_i, cy_i, cz_i, g_i, inv_i)]
    made += [Over(edge, EDGES[0]), Over(edge, EDGES[1])]
    for k, (fields, inside) in enumerate(layers):
        lo, hi, face = none12, none12, None
        if 1 <= k < 6:
            at = (k - 1) % 3, pl.ds(12 * ((k - 1) // 3), 12)
            lo, hi, here = left(*at), right(*at), hit & inside
        else:
            dst, at = (0, 0) if k == 0 else (1, 12)
            face, here = left(dst, pl.ds(at, 12))[11:12], hit & inside & own_row
        values = ring_layer(fields, diag[k], lo, hi, here, face)
        for out, value in zip(made, values):
            out[k if k < 4 else k + 15] = value
        for out, value in zip((cx_o, cy_o, cz_o, g_o, inv_o), values):
            out[k] = value
    cx, cy, cz, g, inv, r, u0 = made
    u1, u2 = Over(edge, EDGES[2]), Over(edge, EDGES[3])

    lanes, rows = sum_lanes(False), sum_rows(False)
    crow, clane = iota((8, 128), 0), iota((8, 128), 1)
    own = (crow < 4) & (clane < 64)
    mask = active[...]
    tails = [sum(cy[4 * a + 3 + k][SIDE:] for k in range(4)) for a in range(4)]
    below = by_right(jnp.concatenate([cx[2][:SIDE]] + tails, axis=0), lanes)
    below_x = by_left(rows, below[:SIDE])
    inverse, uppers, tiles = [], [], []
    for a in range(4):
        below_y = back(below[SIDE + 8 * a : SIDE + 8 * a + 8], 0)
        cx_c, cy_c, cz_c, ab_c = (coarse[n, a] for n in range(4))
        total = cx_c + cy_c + cz_c + ab_c + back(cz_c, 1)
        total = total + (below_x if a == 0 else coarse[0, a - 1])
        total = total + jnp.where(crow == 0, below_y, back(cy_c, 0))
        weight[a] = jnp.where(own, total, 0.0)
        inverse.append(jnp.where(own, mask / jnp.where(own, total, 1.0), 0.0))
        lower = cx_c + pltpu.roll(cy_c, 64, 1)
        tiles.append(pltpu.roll(inverse[a], 64, 1) + pltpu.roll(lower, 4, 0))
        uppers.append(jnp.where(clane == 63, 0.0, cz_c))
    packed[4] = join(uppers)

    for i in (1, 2, 3, 4, 18, 19, 20):
        v = r[i] - (g[i] * u0[i] - near(i, u0, cx, cy, cz))
        r[i] = v
        u1[i] = m1 * u0[i] + q1 * (inv[i] * v)
    for i in (2, 3, 4, 5, 17, 18, 19):
        v = r[i] - (g[i] * u1[i] - near(i, u1, cx, cy, cz))
        r[i] = v
        u2[i] = m2 * u1[i] + q2 * (inv[i] * v)
    for k, i in enumerate((3, 4, 5, 17, 18)):
        iterate[k] = (u0[i] + u1[i] + u2[i])[:SIDE]
    edges = {}
    for k, i in enumerate((3, 4, 5, 6, 16, 17, 18)):
        edges[i - 3] = (r[i] - (g[i] * u2[i] - near(i, u2, cx, cy, cz)))[:SIDE]
        resid[k] = edges[i - 3]
    even = flags[5] > 0
    rest = [edges[x] if x in edges else resid_i[x - 4] for x in range(SIDE)]
    totals = [(rest[x] + rest[x + 1]) + (rest[x + 2] + rest[x + 3]) for x in range(0, SIDE, 4)]

    for k in range(2):
        up, down = edges[14 + k], edges[k]
        for n in range(4):
            ys, zs = 8 * (n // 2), 128 * (n % 2)
            p, q = up[ys : ys + 8, zs : zs + 128], down[ys : ys + 8, zs : zs + 128]
            first[4 * k + n] = jnp.where(even, p, q)
            second[4 * k + n] = jnp.where(even, q, p)
    rhs = by_right(jnp.concatenate(totals, axis=0), lanes)
    for a in range(4):
        tiles[a] = tiles[a] + inverse[a] * by_left(rows, rhs[SIDE * a : SIDE * a + SIDE])
        packed[a] = tiles[a]
    ups, downs = tiles[1:4] + [join(uppers[1:4])], tiles[0:3] + [join(uppers[0:3])]
    for k, (p, q) in enumerate(zip(ups, downs)):
        first[8 + k] = jnp.where(even, p, q)
        second[8 + k] = jnp.where(even, q, p)


def pack_third(flags, resid_i, resid_o, packed, one_x, two_x, first, second):
    even = flags[4] > 0
    low, high = sides(one_x, two_x, flags[5] > 0, flags[0] > 0, flags[1] > 0)

    def edges(x):
        if x < 0 or x >= SIDE:
            get, k = (low, x + 2) if x < 0 else (high, x - SIDE)
            halves = [[get(4 * k + 2 * h + c) for c in range(2)] for h in range(2)]
            return [half[0:2] for half in halves[0]], [half[6:8] for half in halves[1]]
        mine = own_layer(x, resid_i, resid_o, 4, 12, 9)
        halves = [mine[:, 128 * c : 128 * c + 128] for c in range(2)]
        return [half[0:2] for half in halves], [half[14:16] for half in halves]

    for n in range(5):
        parts = [edges(4 * n - 2 + k) for k in range(4)]
        for c in range(2):
            bottom = jnp.concatenate([p[0][c] for p in parts], axis=0)
            top = jnp.concatenate([p[1][c] for p in parts], axis=0)
            first[2 * n + c] = jnp.where(even, top, bottom)
            second[2 * n + c] = jnp.where(even, bottom, top)
    tiles = [low(8 + a) for a in range(3)] + [packed[a] for a in range(4)] + [high(8 + a) for a in range(3)]
    for a, tile in enumerate(tiles + [low(11), packed[4], high(11)]):
        first[10 + a] = tile
        second[10 + a] = tile


def krylov(flags, packed, weight, one_x, two_x, one, two, basis, message, ext, t1s):
    low, high = sides(one_x, two_x, flags[5] > 0, flags[0] > 0, flags[1] > 0)
    left, right = sides(one, two, flags[4] > 0, flags[2] > 0, flags[3] > 0)
    crow, clane = iota((8, 128), 0), iota((8, 128), 1)
    own = (crow < 4) & (clane < 64)

    def unpack(tiles, a):
        turned = pltpu.roll(tiles[a], 4, 0)
        five = [tiles[a], pltpu.roll(tiles[a], 64, 1), turned, pltpu.roll(turned, 64, 1)]
        group, k = (0, a) if a < 3 else (1, a - 3) if a < 7 else (2, a - 7)
        upper = tiles[10 + group]
        upper = pltpu.roll(upper, 4, 0) if k % 2 else upper
        five.append(pltpu.roll(upper, 64, 1) if k >= 2 else upper)
        return [jnp.where(own, v, 0.0) for v in five]

    mine = [low(8 + a) for a in range(3)] + [packed[a] for a in range(4)] + [high(8 + a) for a in range(3)]
    mine = mine + [low(11), packed[4], high(11)]
    previous, following = [left(10 + a) for a in range(13)], [right(10 + a) for a in range(13)]
    for a in range(10):
        here, before, after = unpack(mine, a), unpack(previous, a), unpack(following, a)
        for n in range(5):
            ext[n, a, 0:8] = here[n] + pltpu.roll(after[n], 4, 0)
            ext[n, a, 8:16] = pltpu.roll(before[n], 4, 0)

    z, inv, cx, cy, cz = (ext.at[n] for n in range(5))
    for a in range(1, 9):
        t1s[a] = z[a] - inv[a] * near(a, z, cx, cy, cz)
    for a in range(2, 8):
        t1 = t1s[a]
        basis[0, a - 2] = z[a]
        basis[1, a - 2] = t1
        basis[2, a - 2] = t1 - inv[a] * near(a, t1s, cx, cy, cz)

    def total(parts):
        return jnp.sum(sum(parts), keepdims=True)

    g = [weight[a] for a in range(4)]
    v0, v1, v2 = ([basis[n, a + 1, 0:8] for a in range(4)] for n in range(3))
    s00 = total([w * p * p for w, p in zip(g, v0)])
    s01 = total([w * p * q for w, p, q in zip(g, v0, v1)])
    alpha = jnp.where(s00 > 0, s01 / jnp.where(s00 > 0, s00, 1.0), 0.0)
    e = [q - alpha * p for p, q in zip(v0, v1)]
    te = [q - alpha * p for p, q in zip(v1, v2)]
    terms = [
        total([w * p * p for w, p in zip(g, e)]),
        2.0 * total([w * p * q for w, p, q in zip(g, e, v0)]),
        s00,
        total([w * p * q for w, p, q in zip(g, e, te)]),
        total([w * (p * q + r * t) for w, p, q, r, t in zip(g, v0, te, e, v1)]),
        s01,
    ]
    lane = iota((8, 128), 1)
    line = jnp.where(lane < 64, 0.0, alpha)
    for n, term in enumerate(terms):
        line = jnp.where(lane == n, term, line)
    message[...] = jnp.broadcast_to(line[0:1], (256, 128))


def finish(
    flags, gathered, basis, cx_i, cy_i, cz_i, g_i, inv_i, cx_o, cy_o, cz_o, g_o, inv_o,
    resid_i, resid_o, iterate_i, iterate_o, one_x, two_x, one, two,
    out, correction, lift, u0, u1, r0,
):
    center, m1, q1, m2, q2 = FINE
    low, high = sides(one_x, two_x, flags[5] > 0, flags[0] > 0, flags[1] > 0)
    left, right = sides(one, two, flags[4] > 0, flags[2] > 0, flags[3] > 0)

    pairs = (cx_i, cx_o), (cy_i, cy_o), (cz_i, cz_o), (g_i, g_o), (inv_i, inv_o)
    cx, cy, cz, g, inv = (Layers(*pair) for pair in pairs)

    lines = gathered[...]
    lane1 = iota((1, 128), 1)
    sums = jnp.sum(lines, axis=0, keepdims=True)

    def pick(values, first, count):
        hit = (lane1 >= first) & (lane1 < first + count)
        return jnp.sum(jnp.where(hit, values, 0.0), axis=1, keepdims=True)

    norm = pick(sums, 2, 1)
    a1 = pick(sums, 5, 1) / norm
    shift = pltpu.roll(lines, 64, 1) - a1
    plain, linear, quadratic = (((lane1 == k) | (lane1 == k + 3)).astype(f32) for k in range(3))
    power = plain + shift * (linear + shift * quadratic)
    sums = jnp.sum(lines * power, axis=0, keepdims=True)
    square, energy = pick(sums, 0, 3), pick(sums, 3, 3)
    bound = jnp.maximum(a1, energy / square) + jnp.sqrt(square / norm)
    middle, k1, h1, k2, h2 = factors(coarse_share, 1.0)
    scale = 1.0 / bound
    v0, h1, h2 = scale * (1.0 / middle), scale * h1, scale * h2
    v1 = (k1 * v0 + h1, -h1 * v0)
    v2 = (k2 * v1[0] + h2, k2 * v1[1] - h2 * (v0 + v1[0]), -h2 * v1[1])
    weights = (v0 + v1[0] + v2[0], v1[1] + v2[1], v2[2])

    upper = iota((8, 128), 0) < 4
    tall = []
    for a in range(6):
        field = weights[0] * basis[0, a] + weights[1] * basis[1, a] + weights[2] * basis[2, a]
        if 1 <= a <= 4:
            correction[a - 1] = field[0:4, 0:64]
        for p, q in ((0, 1), (2, 3), (4, 15)):
            p, q = (jnp.broadcast_to(field[k : k + 1], (8, 128)) for k in (p, q))
            tall.append(jnp.where(upper, p, q))
    lanes = (iota((128, LONG), 1) // 4 == iota((128, LONG), 0)).astype(bf16)
    fine = by_right(jnp.concatenate(tall, axis=0), lanes)
    lifted = [fine[RING * a : RING * a + RING] for a in range(6)]
    for i in range(ROWS):
        lift[i] = lifted[(i + 1) // 4]

    none4 = jnp.zeros((4, LONG), f32)

    def strip(get, x):
        n, k = x // 4, x % 4
        return jnp.concatenate([get(2 * n + c, pl.ds(2 * k, 2)) for c in range(2)], axis=1)

    for i in range(1, ROWS - 1):
        x = i - 1
        if x < 2 or x >= 18:
            get, k = (low, x) if x < 2 else (high, x - 18)
            halves = [
                jnp.concatenate([get(4 * k + 2 * h + c) for c in range(2)], axis=1) for h in range(2)
            ]
            mine = jnp.concatenate(halves, axis=0)
        else:
            mine = own_layer(x - 2, resid_i, resid_o, 4, 12, 9)
        r0[i] = jnp.concatenate([mine, strip(right, x), none4, strip(left, x)], axis=0)

    for i in range(1, ROWS - 1):
        r = r0[i] - (g[i] * lift[i] - near(i, lift, cx, cy, cz))
        r0[i] = r
        u0[i] = inv[i] * r * (1.0 / center)

    for i in range(2, ROWS - 2):
        u = u0[i]
        r = r0[i] - (g[i] * u - near(i, u0, cx, cy, cz))
        r0[i] = r
        u1[i] = m1 * u + q1 * (inv[i] * r)

    for i in range(3, 19):
        u = u1[i]
        r = r0[i] - (g[i] * u - near(i, u1, cx, cy, cz))
        step = (u0[i] + u) + (m2 * u + q2 * (inv[i] * r)) + lift[i]
        out[i - 3] = own_layer(i - 3, iterate_i, iterate_o, 3, 13, 11) + step[:SIDE]


def swap(values, axis, odd):
    count = lax.axis_size(axis)
    other = [(i ^ 1) if not odd else (((i + 1) ^ 1) - 1) % count for i in range(count)]
    return lax.ppermute(values, axis, list(enumerate(other)))


def body(src, cx, cy, cz, ab, active):
    ix, iy = lax.axis_index("coarse"), lax.axis_index("fine")
    nx, ny = lax.axis_size("coarse"), lax.axis_size("fine")
    flags = jnp.stack([ix > 0, ix < nx - 1, iy > 0, iy < ny - 1, iy % 2 == 0, ix % 2 == 0]).astype(jnp.int32)
    block, ring = (SIDE, SIDE, LONG), pltpu.VMEM((ROWS, RING, LONG), f32)

    first, second = pack_first_call((src, cx, cy, cz, ab))
    one_x, two_x = swap(first, "coarse", False), swap(second, "coarse", True)
    coarse, mask = call(coarsen, [(4, 4, 8, 128), (8, 128)], ins=[VMEM] * 5)(cx, cy, cz, ab, active)
    diag, first, second = call(
        pack_inner, [block, (8, 24, LONG), (8, 24, LONG)], ins=[SMEM] + [VMEM] * 5
    )(flags, src, cx, cy, cz, ab)
    one, two = swap(first, "fine", False), swap(second, "fine", True)
    diag_out, first, second = call(
        pack_outer, [(7, SIDE, LONG), (3, 24, LONG), (3, 24, LONG)], ins=[SMEM] + [VMEM] * 7
    )(flags, src, cx, cy, cz, ab, one_x, two_x)
    one_out, two_out = swap(first, "fine", False), swap(second, "fine", True)
    inner, outer = (15, RING, LONG), (7, RING, LONG)
    *fields_i, edge, iterate_i, resid_i = call(
        smooth_inner,
        [inner] * 5 + [(18, RING, LONG), (11, SIDE, LONG), (9, SIDE, LONG)],
        [pltpu.VMEM(inner, f32)] * 4,
        ins=[SMEM] + [VMEM] * 7,
    )(flags, src, cx, cy, cz, diag, one, two)
    *fields_o, iterate_o, resid_o, packed, weight, first, second = call(
        smooth_outer,
        [outer] * 5 + [(5, SIDE, LONG), (7, SIDE, LONG)]
        + [(5, 8, 128), (4, 8, 128), (12, 8, 128), (12, 8, 128)],
        ins=[SMEM] + [VMEM] * 18,
    )(
        flags, src, cx, cy, cz, one_x, two_x, diag_out, one_out, two_out, coarse, mask,
        *fields_i, edge, resid_i,
    )
    one_x, two_x = swap(first, "coarse", False), swap(second, "coarse", True)
    first, second = call(pack_third, [(23, 8, 128)] * 2, ins=[SMEM] + [VMEM] * 5)(
        flags, resid_i, resid_o, packed, one_x, two_x
    )
    one, two = swap(first, "fine", False), swap(second, "fine", True)
    count = nx * ny
    basis, message = call(
        krylov,
        [(3, 6, 16, 128), (256, 128)],
        [pltpu.VMEM((5, 10, 16, 128), f32), pltpu.VMEM((10, 16, 128), f32)],
        ins=[SMEM] + [VMEM] * 6,
    )(flags, packed, weight, one_x, two_x, one, two)
    gathered = lax.all_to_all(message[:count], ("coarse", "fine"), 0, 0, tiled=True)
    out, correction = call(
        finish,
        [block, (4, 4, 64)],
        [ring] * 4,
        ins=[SMEM] + [VMEM] * 20,
    )(
        flags, gathered, basis, *fields_i, *fields_o, resid_i, resid_o, iterate_i, iterate_o,
        one_x, two_x, one, two,
    )
    return (out, correction)


def solution(mesh):
    spec = P("coarse", "fine", None)
    return jax.shard_map(
        body, mesh=mesh, in_specs=(spec,) * 6, out_specs=(spec,) * 2, check_vma=False
    )
```

profile of v0, /device:TPU:1, one launch (start us, length us, event | category | flops | bytes accessed | tf_op | source)
XLA Modules:
  0.0 66.5 jit_solution(6705424831973994072)
XLA Ops:
  0.6 0.0 copy-start
  0.6 0.0 copy-start.1
  0.7 0.0 copy-start.2
  0.7 0.0 copy-start.3
  0.7 0.0 copy-start.4
  0.7 2.0 %shard_map.77 = (f32[16,16,256]{2,1,0:T(8,128)}, f32[16,16,256]{2,1,0:T(8,128)}) custom-call(f32[16,16,256]{2,1,0:T(8,128)} %src.7, f32[16,16,256]{2,1,0:T(8,128)} %cx.9, f32[16,16,256]{2,1,0:T(8,128)} %cy.9, f32[16,16,256]{2,1,0:T(8,128)} %cz.9, f32[16,16,256]{2,1,0:T(8,128)} %ab.5), custom_call_target="tpu_custom_call" | custom-call | tf_op jit(solution)/shard_map/pallas_call | solution.py:85
  2.7 3.3 %collective-permute-start = (f32[16,16,256]{2,1,0:T(8,128)}, f32[16,16,256]{2,1,0:T(8,128)S(1)}, u32[]{:S(2)}, u32[]{:S(2)}) collective-permute-start(f32[16,16,256]{2,1,0:T(8,128)} %get-tuple-element.35), channel_id=1, source_target_pairs={{0,16},{16,0},{32,48},{48,32},{64,80},{80,64},{96,112},{112,96},{1... | collective-permute-start | bytes 786440 | tf_op jit(solution)/shard_map/ppermute | solution.py:577
  6.0 0.0 collective-permute-start.1
  6.0 0.1 stack.27
  6.1 0.0 copy-done
  6.1 0.0 copy-done.1
  6.1 0.0 copy-done.2
  6.1 0.0 copy-done.3
  6.2 0.0 copy-done.4
  6.2 0.8 %shard_map.80 = (f32[16,16,256]{2,1,0:T(8,128)S(1)}, f32[8,24,256]{2,1,0:T(8,128)S(1)}, f32[8,24,256]{2,1,0:T(8,128)S(1)}) custom-call(s32[6]{0:T(128)S(1)} %convert_element_type.3.flags, f32[16,16,256]{2,1,0:T(8,128)S(1)} %copy-done.3, f32[16,16,256]{2,1,0:T(8,128)S(1)} %copy-done, f32[16,16,256]{2,1,0:T(8,128)S(1)} %copy-done.1, ...), custom_call_target="tpu_custom_call" | custom-call | tf_op jit(solution)/shard_map/pallas_call | solution.py:589
  7.0 1.2 %collective-permute-start.4 = (f32[8,24,256]{2,1,0:T(8,128)S(1)}, f32[8,24,256]{2,1,0:T(8,128)S(1)}, u32[]{:S(2)}, u32[]{:S(2)}) collective-permute-start(f32[8,24,256]{2,1,0:T(8,128)S(1)} %get-tuple-element.43), channel_id=1, source_target_pairs={{0,1},{1,0},{2,3},{3,2},{4,5},{5,4},{6,7},{7,6},{8,9},{9,8},{10,11... | collective-permute-start | bytes 589832 | tf_op jit(solution)/shard_map/ppermute | solution.py:577
  8.1 4.3 %collective-permute-start.5 = (f32[8,24,256]{2,1,0:T(8,128)S(1)}, f32[8,24,256]{2,1,0:T(8,128)S(1)}, u32[]{:S(2)}, u32[]{:S(2)}) collective-permute-start(f32[8,24,256]{2,1,0:T(8,128)S(1)} %get-tuple-element.44), channel_id=1, source_target_pairs={{0,15},{1,2},{2,1},{3,4},{4,3},{5,6},{6,5},{7,8},{8,7},{9,10},{10,... | collective-permute-start | bytes 589832 | tf_op jit(solution)/shard_map/ppermute | solution.py:577
  12.4 0.0 collective-permute-done.one.one_x
  12.4 0.0 collective-permute-done.1.two.two_x
  12.4 0.7 %shard_map.78 = (f32[7,16,256]{2,1,0:T(8,128)S(1)}, f32[3,24,256]{2,1,0:T(8,128)S(1)}, f32[3,24,256]{2,1,0:T(8,128)S(1)}) custom-call(s32[6]{0:T(128)S(1)} %convert_element_type.3.flags, f32[16,16,256]{2,1,0:T(8,128)S(1)} %copy-done.3, f32[16,16,256]{2,1,0:T(8,128)S(1)} %copy-done, f32[16,16,256]{2,1,0:T(8,128)S(1)} %copy-done.1, ...), custom_call_target="tpu_custom_call" | custom-call | tf_op jit(solution)/shard_map/pallas_call | solution.py:593
  13.1 0.0 copy-start.5
  13.1 0.1 collective-permute-start.2
  13.2 3.3 %collective-permute-start.3 = (f32[3,24,256]{2,1,0:T(8,128)S(1)}, f32[3,24,256]{2,1,0:T(8,128)S(1)}, u32[]{:S(2)}, u32[]{:S(2)}) collective-permute-start(f32[3,24,256]{2,1,0:T(8,128)S(1)} %get-tuple-element.39), channel_id=1, source_target_pairs={{0,15},{1,2},{2,1},{3,4},{4,3},{5,6},{6,5},{7,8},{8,7},{9,10},{10,... | collective-permute-start | bytes 221192 | tf_op jit(solution)/shard_map/ppermute | solution.py:577
  16.5 0.0 copy-done.5
  16.5 0.9 %shard_map.79 = (f32[4,4,8,128]{3,2,1,0:T(8,128)S(1)}, f32[8,128]{1,0:T(8,128)S(1)}) custom-call(f32[16,16,256]{2,1,0:T(8,128)S(1)} %copy-done, f32[16,16,256]{2,1,0:T(8,128)S(1)} %copy-done.1, f32[16,16,256]{2,1,0:T(8,128)S(1)} %copy-done.2, f32[16,16,256]{2,1,0:T(8,128)S(1)} %copy-done.4, s32[1,1,16]{2,1,0:T(1,128)S(1)} %copy-done.5), custom_call_target="tpu_custom_call" | custom-call | tf_op jit(solution)/shard_map/pallas_call | solution.py:588
  17.4 0.0 collective-permute-done.4.one
  17.5 0.0 collective-permute-done.5.two
  17.5 1.5 %shard_map.81 = (f32[15,24,256]{2,1,0:T(8,128)S(1)}, f32[15,24,256]{2,1,0:T(8,128)S(1)}, f32[15,24,256]{2,1,0:T(8,128)S(1)}, f32[15,24,256]{2,1,0:T(8,128)S(1)},...) custom-call(s32[6]{0:T(128)S(1)} %convert_element_type.3.flags, ...), custom_call_target="tpu_custom_call" | custom-call | tf_op jit(solution)/shard_map/pallas_call | solution.py:598
  19.0 0.0 collective-permute-done.2.one
  19.0 1.8 %collective-permute-done.3.two = f32[3,24,256]{2,1,0:T(8,128)S(1)} collective-permute-done((f32[3,24,256]{2,1,0:T(8,128)S(1)}, f32[3,24,256]{2,1,0:T(8,128)S(1)}, u32[]{:S(2)}, u32[]{:S(2)}) %collective-permute-start.3) | collective-permute-done | bytes 73760 | tf_op jit(solution)/shard_map/ppermute | solution.py:577
  20.9 1.5 %shard_map.82 = (f32[7,24,256]{2,1,0:T(8,128)S(1)}, f32[7,24,256]{2,1,0:T(8,128)S(1)}, f32[7,24,256]{2,1,0:T(8,128)S(1)}, f32[7,24,256]{2,1,0:T(8,128)S(1)}, f32...) custom-call(s32[6]{0:T(128)S(1)} %convert_element_type.3.flags, ...), custom_call_target="tpu_custom_call" | custom-call | tf_op jit(solution)/shard_map/pallas_call | solution.py:604
  22.4 5.1 %collective-permute-start.6 = (f32[12,8,128]{2,1,0:T(8,128)S(1)}, f32[12,8,128]{2,1,0:T(8,128)S(1)}, u32[]{:S(2)}, u32[]{:S(2)}) collective-permute-start(f32[12,8,128]{2,1,0:T(8,128)S(1)} %get-tuple-element.54), channel_id=1, source_target_pairs={{0,16},{16,0},{32,48},{48,32},{64,80},{80,64},{96,112},{112,96},{1... | collective-permute-start | bytes 147464 | tf_op jit(solution)/shard_map/ppermute | solution.py:577
  27.4 0.0 collective-permute-start.7
  27.4 0.9 %collective-permute-done.6.one_x = f32[12,8,128]{2,1,0:T(8,128)S(1)} collective-permute-done((f32[12,8,128]{2,1,0:T(8,128)S(1)}, f32[12,8,128]{2,1,0:T(8,128)S(1)}, u32[]{:S(2)}, u32[]{:S(2)}) %collective-permute-start.6) | collective-permute-done | bytes 49184 | tf_op jit(solution)/shard_map/ppermute | solution.py:577
  28.3 2.6 %collective-permute-done.7.two_x = f32[12,8,128]{2,1,0:T(8,128)S(1)} collective-permute-done((f32[12,8,128]{2,1,0:T(8,128)S(1)}, f32[12,8,128]{2,1,0:T(8,128)S(1)}, u32[]{:S(2)}, u32[]{:S(2)}) %collective-permute-start.7) | collective-permute-done | bytes 49184 | tf_op jit(solution)/shard_map/ppermute | solution.py:577
  31.0 0.6 shard_map.83
  31.5 0.1 collective-permute-start.8
  31.6 2.9 %collective-permute-start.9 = (f32[23,8,128]{2,1,0:T(8,128)S(1)}, f32[23,8,128]{2,1,0:T(8,128)S(1)}, u32[]{:S(2)}, u32[]{:S(2)}) collective-permute-start(f32[23,8,128]{2,1,0:T(8,128)S(1)} %get-tuple-element.58), channel_id=1, source_target_pairs={{0,15},{1,2},{2,1},{3,4},{4,3},{5,6},{6,5},{7,8},{8,7},{9,10},{10,... | collective-permute-start | bytes 282632 | tf_op jit(solution)/shard_map/ppermute | solution.py:577
  34.6 0.5 collective-permute-done.8.one
  35.0 3.4 %collective-permute-done.9.two = f32[23,8,128]{2,1,0:T(8,128)S(1)} collective-permute-done((f32[23,8,128]{2,1,0:T(8,128)S(1)}, f32[23,8,128]{2,1,0:T(8,128)S(1)}, u32[]{:S(2)}, u32[]{:S(2)}) %collective-permute-start.9) | collective-permute-done | bytes 94240 | tf_op jit(solution)/shard_map/ppermute | solution.py:577
  38.5 1.0 %shard_map.84 = (f32[3,6,16,128]{3,2,1,0:T(8,128)S(1)}, f32[256,128]{1,0:T(8,128)S(1)}) custom-call(s32[6]{0:T(128)S(1)} %convert_element_type.3.flags, f32[5,8,128]{2,1,0:T(8,128)S(1)} %get-tuple-element.52.packed, f32[4,8,128]{2,1,0:T(8,128)S(1)} %get-tuple-element.53.weight, f32[12,8,128]{2,1,0:T(8,128)S(1)} %collective-permute-done.6.one_x, ...), custom_call_target="tpu_custom_call" | custom-call | tf_op jit(solution)/shard_map/pallas_call | solution.py:619
  39.5 24.1 %all_to_all.11 = f32[256,1,128]{2,1,0:T(1,128)S(1)} all-to-all(f32[256,1,128]{2,1,0:T(1,128)S(1)} %bitcast.11), channel_id=1, replica_groups=mesh['coarse'=16,'fine'=16] {'coarse','fine'}, dimensions={0} | all-to-all | bytes 262144 | tf_op jit(solution)/shard_map/all_to_all | solution.py:625
  63.5 3.0 %shard_map.85 = (f32[16,16,256]{2,1,0:T(8,128)}, f32[4,4,64]{2,1,0:T(4,128)}) custom-call(s32[6]{0:T(128)S(1)} %convert_element_type.3.flags, f32[256,128]{1,0:T(8,128)S(1)} %bitcast.10, f32[3,6,16,128]{3,2,1,0:T(8,128)S(1)} %get-tuple-element.60.basis, f32[15,24,256]{2,1,0:T(8,128)S(1)} %get-tuple-element.45.cx_i, ...), custom_call_target="tpu_custom_call" | custom-call | tf_op jit(solution)/shard_map/pallas_call | solution.py:626
  (1 shorter events, 0.0 us)
Async XLA Ops:
  0.6 5.5 %copy-start = (f32[16,16,256]{2,1,0:T(8,128)S(1)}, f32[16,16,256]{2,1,0:T(8,128)}, u32[]{:S(2)}) copy-start(f32[16,16,256]{2,1,0:T(8,128)} %cx.9) | copy-start | bytes 786436
  0.6 5.5 %copy-start.1 = (f32[16,16,256]{2,1,0:T(8,128)S(1)}, f32[16,16,256]{2,1,0:T(8,128)}, u32[]{:S(2)}) copy-start(f32[16,16,256]{2,1,0:T(8,128)} %cy.9) | copy-start | bytes 786436
  0.7 5.5 %copy-start.2 = (f32[16,16,256]{2,1,0:T(8,128)S(1)}, f32[16,16,256]{2,1,0:T(8,128)}, u32[]{:S(2)}) copy-start(f32[16,16,256]{2,1,0:T(8,128)} %cz.9) | copy-start | bytes 786436
  0.7 5.5 %copy-start.3 = (f32[16,16,256]{2,1,0:T(8,128)S(1)}, f32[16,16,256]{2,1,0:T(8,128)}, u32[]{:S(2)}) copy-start(f32[16,16,256]{2,1,0:T(8,128)} %src.7) | copy-start | bytes 786436
  0.7 5.5 %copy-start.4 = (f32[16,16,256]{2,1,0:T(8,128)S(1)}, f32[16,16,256]{2,1,0:T(8,128)}, u32[]{:S(2)}) copy-start(f32[16,16,256]{2,1,0:T(8,128)} %ab.5) | copy-start | bytes 786436
  2.7 9.7 %collective-permute-start = (f32[16,16,256]{2,1,0:T(8,128)}, f32[16,16,256]{2,1,0:T(8,128)S(1)}, u32[]{:S(2)}, u32[]{:S(2)}) collective-permute-start(f32[16,16,256]{2,1,0:T(8,128)} %get-tuple-element.35), channel_id=1, source_target_pairs={{0,16},{16,0},{32,48},{48,32},{64,80},{80,64},{96,112},{112,96},{1... | collective-permute-start | bytes 786440 | tf_op jit(solution)/shard_map/ppermute | solution.py:577
  6.0 6.4 %collective-permute-start.1 = (f32[16,16,256]{2,1,0:T(8,128)}, f32[16,16,256]{2,1,0:T(8,128)S(1)}, u32[]{:S(2)}, u32[]{:S(2)}) collective-permute-start(f32[16,16,256]{2,1,0:T(8,128)} %get-tuple-element.36), channel_id=1, source_target_pairs={{0,240},{16,32},{32,16},{48,64},{64,48},{80,96},{96,80},{112,128},... | collective-permute-start | bytes 786440 | tf_op jit(solution)/shard_map/ppermute | solution.py:577
  7.0 10.5 %collective-permute-start.4 = (f32[8,24,256]{2,1,0:T(8,128)S(1)}, f32[8,24,256]{2,1,0:T(8,128)S(1)}, u32[]{:S(2)}, u32[]{:S(2)}) collective-permute-start(f32[8,24,256]{2,1,0:T(8,128)S(1)} %get-tuple-element.43), channel_id=1, source_target_pairs={{0,1},{1,0},{2,3},{3,2},{4,5},{5,4},{6,7},{7,6},{8,9},{9,8},{10,11... | collective-permute-start | bytes 589832 | tf_op jit(solution)/shard_map/ppermute | solution.py:577
  8.1 9.3 %collective-permute-start.5 = (f32[8,24,256]{2,1,0:T(8,128)S(1)}, f32[8,24,256]{2,1,0:T(8,128)S(1)}, u32[]{:S(2)}, u32[]{:S(2)}) collective-permute-start(f32[8,24,256]{2,1,0:T(8,128)S(1)} %get-tuple-element.44), channel_id=1, source_target_pairs={{0,15},{1,2},{2,1},{3,4},{4,3},{5,6},{6,5},{7,8},{8,7},{9,10},{10,... | collective-permute-start | bytes 589832 | tf_op jit(solution)/shard_map/ppermute | solution.py:577
  13.1 3.5 %copy-start.5 = (s32[1,1,16]{2,1,0:T(1,128)S(1)}, s32[1,1,16]{2,1,0:T(1,128)}, u32[]{:S(2)}) copy-start(s32[1,1,16]{2,1,0:T(1,128)} %active.1) | copy-start | bytes 196
  13.1 5.9 %collective-permute-start.2 = (f32[3,24,256]{2,1,0:T(8,128)S(1)}, f32[3,24,256]{2,1,0:T(8,128)S(1)}, u32[]{:S(2)}, u32[]{:S(2)}) collective-permute-start(f32[3,24,256]{2,1,0:T(8,128)S(1)} %get-tuple-element.38), channel_id=1, source_target_pairs={{0,1},{1,0},{2,3},{3,2},{4,5},{5,4},{6,7},{7,6},{8,9},{9,8},{10,11... | collective-permute-start | bytes 221192 | tf_op jit(solution)/shard_map/ppermute | solution.py:577
  13.2 7.7 %collective-permute-start.3 = (f32[3,24,256]{2,1,0:T(8,128)S(1)}, f32[3,24,256]{2,1,0:T(8,128)S(1)}, u32[]{:S(2)}, u32[]{:S(2)}) collective-permute-start(f32[3,24,256]{2,1,0:T(8,128)S(1)} %get-tuple-element.39), channel_id=1, source_target_pairs={{0,15},{1,2},{2,1},{3,4},{4,3},{5,6},{6,5},{7,8},{8,7},{9,10},{10,... | collective-permute-start | bytes 221192 | tf_op jit(solution)/shard_map/ppermute | solution.py:577
  22.4 5.9 %collective-permute-start.6 = (f32[12,8,128]{2,1,0:T(8,128)S(1)}, f32[12,8,128]{2,1,0:T(8,128)S(1)}, u32[]{:S(2)}, u32[]{:S(2)}) collective-permute-start(f32[12,8,128]{2,1,0:T(8,128)S(1)} %get-tuple-element.54), channel_id=1, source_target_pairs={{0,16},{16,0},{32,48},{48,32},{64,80},{80,64},{96,112},{112,96},{1... | collective-permute-start | bytes 147464 | tf_op jit(solution)/shard_map/ppermute | solution.py:577
  27.4 3.5 %collective-permute-start.7 = (f32[12,8,128]{2,1,0:T(8,128)S(1)}, f32[12,8,128]{2,1,0:T(8,128)S(1)}, u32[]{:S(2)}, u32[]{:S(2)}) collective-permute-start(f32[12,8,128]{2,1,0:T(8,128)S(1)} %get-tuple-element.55), channel_id=1, source_target_pairs={{0,240},{16,32},{32,16},{48,64},{64,48},{80,96},{96,80},{112,128},... | collective-permute-start | bytes 147464 | tf_op jit(solution)/shard_map/ppermute | solution.py:577
  31.5 3.5 %collective-permute-start.8 = (f32[23,8,128]{2,1,0:T(8,128)S(1)}, f32[23,8,128]{2,1,0:T(8,128)S(1)}, u32[]{:S(2)}, u32[]{:S(2)}) collective-permute-start(f32[23,8,128]{2,1,0:T(8,128)S(1)} %get-tuple-element.57), channel_id=1, source_target_pairs={{0,1},{1,0},{2,3},{3,2},{4,5},{5,4},{6,7},{7,6},{8,9},{9,8},{10,11... | collective-permute-start | bytes 282632 | tf_op jit(solution)/shard_map/ppermute | solution.py:577
  31.6 6.8 %collective-permute-start.9 = (f32[23,8,128]{2,1,0:T(8,128)S(1)}, f32[23,8,128]{2,1,0:T(8,128)S(1)}, u32[]{:S(2)}, u32[]{:S(2)}) collective-permute-start(f32[23,8,128]{2,1,0:T(8,128)S(1)} %get-tuple-element.58), channel_id=1, source_target_pairs={{0,15},{1,2},{2,1},{3,4},{4,3},{5,6},{6,5},{7,8},{8,7},{9,10},{10,... | collective-permute-start | bytes 282632 | tf_op jit(solution)/shard_map/ppermute | solution.py:577
where the time goes:
time: 66.6 us; the launch traced here: 66.5 us
  blocking collectives  24.1 us (36%)
  starting transfers between devices  20.3 us (30%)
  Pallas kernels  11.9 us (18%)
  waiting for transfers between devices  9.28 us (14%)
  between operations  0.8 us (1%)
    all_to_all x1, blocking collectives, body(): lax.all_to_all(message[:count], ('coarse', 'fine'), 0, 0, tiled=True)  24.1 us
    ppermute x10, starting transfers between devices, swap(): return lax.ppermute(values, axis, list(enumerate(other)))  20.3 us
    ppermute x10, waiting for transfers between devices, swap(): return lax.ppermute(values, axis, list(enumerate(other)))  9.28 us
    pallas_call x1, Pallas kernels, body(): call(finish, [block, (4, 4, 64)], [ring] * 4, ins=[SMEM] + [VMEM] * 20)  2.97 us
    pallas_call x1, Pallas kernels, pack_first_call(): pl.pallas_call(pack_first, out_shape=[jax.ShapeDtypeStruct((16, SIDE, LON...  2.01 us
    pallas_call x1, Pallas kernels, body(): call(smooth_inner, [inner] * 5 + [(18, RING, LONG), (11, SIDE, LONG), (9,...  1.55 us
    pallas_call x1, Pallas kernels, body(): call(smooth_outer, [outer] * 5 + [(5, SIDE, LONG), (7, SIDE, LONG)] + [(5...  1.47 us
  transfers between devices with their start and end apart: 10, of which 5 were waited for; matrix products, arithmetic and copies ran while one was open for 0% of the time, Pallas kernels for 6%

commit v1 on v0

--- a/solution.py
+++ b/solution.py
@@ -401,55 +401,84 @@
         second[8 + k] = jnp.where(even, q, p)
 
 
-def pack_third(flags, resid_i, resid_o, packed, one_x, two_x, first, second):
-    even = flags[4] > 0
+def residual_strips(layers, even, first, second, at):
+    for c in range(2):
+        parts = [layer[c] for layer in layers]
+        bottom = jnp.concatenate([head for head, _ in parts], axis=0)
+        top = jnp.concatenate([tail for _, tail in parts], axis=0)
+        first[at + c] = jnp.where(even, top, bottom)
+        second[at + c] = jnp.where(even, bottom, top)
+
+
+def pack_own(flags, resid_i, resid_o, packed, first, second):
+    def halves(x):
+        mine = own_layer(x, resid_i, resid_o, 4, 12, 9)
+        return [(mine[0:2, at : at + 128], mine[14:16, at : at + 128]) for at in (0, 128)]
+
+    for n in range(4):
+        residual_strips([halves(4 * n + k) for k in range(4)], flags[4] > 0, first, second, 2 * n)
+    for k in range(5):
+        first[8 + k] = packed[k]
+        second[8 + k] = packed[k]
+
+
+def pack_halo(flags, one_x, two_x, first, second):
     low, high = sides(one_x, two_x, flags[5] > 0, flags[0] > 0, flags[1] > 0)
 
-    def edges(x):
-        if x < 0 or x >= SIDE:
-            get, k = (low, x + 2) if x < 0 else (high, x - SIDE)
-            halves = [[get(4 * k + 2 * h + c) for c in range(2)] for h in range(2)]
-            return [half[0:2] for half in halves[0]], [half[6:8] for half in halves[1]]
-        mine = own_layer(x, resid_i, resid_o, 4, 12, 9)
-        halves = [mine[:, 128 * c : 128 * c + 128] for c in range(2)]
-        return [half[0:2] for half in halves], [half[14:16] for half in halves]
-
-    for n in range(5):
-        parts = [edges(4 * n - 2 + k) for k in range(4)]
-        for c in range(2):
-            bottom = jnp.concatenate([p[0][c] for p in parts], axis=0)
-            top = jnp.concatenate([p[1][c] for p in parts], axis=0)
-            first[2 * n + c] = jnp.where(even, top, bottom)
-            second[2 * n + c] = jnp.where(even, bottom, top)
-    tiles = [low(8 + a) for a in range(3)] + [packed[a] for a in range(4)] + [high(8 + a) for a in range(3)]
-    for a, tile in enumerate(tiles + [low(11), packed[4], high(11)]):
-        first[10 + a] = tile
-        second[10 + a] = tile
-
-
-def krylov(flags, packed, weight, one_x, two_x, one, two, basis, message, ext, t1s):
+    def halves(get, k):
+        return [(get(4 * k + c)[0:2], get(4 * k + 2 + c)[6:8]) for c in range(2)]
+
+    layers = [halves(low, 0), halves(low, 1), halves(high, 0), halves(high, 1)]
+    residual_strips(layers, flags[4] > 0, first, second, 0)
+    for k, get in enumerate((low, high)):
+        for a in range(4):
+            at = 2 + 3 * k + a if a < 3 else 8 + k
+            tile = get(8 + a)
+            first[at] = tile
+            second[at] = tile
+
+
+def krylov(flags, packed, weight, one_x, two_x, one, two, one_out, two_out, basis, message, ext, t1s):
     low, high = sides(one_x, two_x, flags[5] > 0, flags[0] > 0, flags[1] > 0)
     left, right = sides(one, two, flags[4] > 0, flags[2] > 0, flags[3] > 0)
+    left_out, right_out = sides(one_out, two_out, flags[4] > 0, flags[2] > 0, flags[3] > 0)
     crow, clane = iota((8, 128), 0), iota((8, 128), 1)
-    own = (crow < 4) & (clane < 64)
-
-    def unpack(tiles, a):
-        turned = pltpu.roll(tiles[a], 4, 0)
-        five = [tiles[a], pltpu.roll(tiles[a], 64, 1), turned, pltpu.roll(turned, 64, 1)]
+    top, thin = crow < 4, clane < 64
+
+    def tiles(own, out):
+        return [out(2 + a) for a in range(3)] + [own(8 + a) for a in range(4)] + [
+            out(5 + a) for a in range(3)
+        ] + [out(8), own(12), out(9)]
+
+    mine = [low(8 + a) for a in range(3)] + [packed[a] for a in range(4)]
+    mine += [high(8 + a) for a in range(3)] + [low(11), packed[4], high(11)]
+    previous, following = tiles(left, left_out), tiles(right, right_out)
+
+    def upper(field, a):
         group, k = (0, a) if a < 3 else (1, a - 3) if a < 7 else (2, a - 7)
-        upper = tiles[10 + group]
-        upper = pltpu.roll(upper, 4, 0) if k % 2 else upper
-        five.append(pltpu.roll(upper, 64, 1) if k >= 2 else upper)
-        return [jnp.where(own, v, 0.0) for v in five]
-
-    mine = [low(8 + a) for a in range(3)] + [packed[a] for a in range(4)] + [high(8 + a) for a in range(3)]
-    mine = mine + [low(11), packed[4], high(11)]
-    previous, following = [left(10 + a) for a in range(13)], [right(10 + a) for a in range(13)]
+        tile = field[10 + group]
+        return (pltpu.roll(tile, 64, 1) if k >= 2 else tile), k % 2
+
+    def turn(tile):
+        return pltpu.roll(tile, 4, 0)
+
     for a in range(10):
-        here, before, after = unpack(mine, a), unpack(previous, a), unpack(following, a)
-        for n in range(5):
-            ext[n, a, 0:8] = here[n] + pltpu.roll(after[n], 4, 0)
-            ext[n, a, 8:16] = pltpu.roll(before[n], 4, 0)
+        here, after, before = mine[a], following[a], previous[a]
+        pairs = (
+            (jnp.where(top, here, turn(after)), jnp.where(top, turn(here), after)),
+            (jnp.where(top, 0.0, turn(before)), jnp.where(top, 0.0, before)),
+        )
+        (here, odd), (after, _), (before, _) = (upper(f, a) for f in (mine, following, previous))
+        if odd:
+            faces = jnp.where(top, turn(here), after), jnp.where(top, 0.0, before)
+        else:
+            faces = jnp.where(top, here, turn(after)), jnp.where(top, 0.0, turn(before))
+        for n in range(2):
+            at = pl.ds(8 * n, 8)
+            for m in range(2):
+                ext[2 * m, a, at] = jnp.where(thin, pairs[n][m], 0.0)
+                ext[2 * m + 1, a, at] = jnp.where(thin, pltpu.roll(pairs[n][m], 64, 1), 0.0)
+            ext[4, a, at] = jnp.where(thin, faces[n], 0.0)
 
     z, inv, cx, cy, cz = (ext.at[n] for n in range(5))
     for a in range(1, 9):
@@ -487,7 +516,7 @@
 
 def finish(
     flags, gathered, basis, cx_i, cy_i, cz_i, g_i, inv_i, cx_o, cy_o, cz_o, g_o, inv_o,
-    resid_i, resid_o, iterate_i, iterate_o, one_x, two_x, one, two,
+    resid_i, resid_o, iterate_i, iterate_o, one_x, two_x, one, two, one_out, two_out,
     out, correction, lift, u0, u1, r0,
 ):
     center, m1, q1, m2, q2 = FINE
@@ -537,8 +566,10 @@
 
     none4 = jnp.zeros((4, LONG), f32)
 
-    def strip(get, x):
-        n, k = x // 4, x % 4
+    left_out, right_out = sides(one_out, two_out, flags[4] > 0, flags[2] > 0, flags[3] > 0)
+
+    def strip(own, outer, x):
+        get, n, k = (own, (x - 2) // 4, (x - 2) % 4) if 2 <= x < 18 else (outer, 0, x if x < 2 else x - 16)
         return jnp.concatenate([get(2 * n + c, pl.ds(2 * k, 2)) for c in range(2)], axis=1)
 
     for i in range(1, ROWS - 1):
@@ -551,7 +582,8 @@
             mine = jnp.concatenate(halves, axis=0)
         else:
             mine = own_layer(x - 2, resid_i, resid_o, 4, 12, 9)
-        r0[i] = jnp.concatenate([mine, strip(right, x), none4, strip(left, x)], axis=0)
+        after, before = strip(right, right_out, x), strip(left, left_out, x)
+        r0[i] = jnp.concatenate([mine, after, none4, before], axis=0)
 
     for i in range(1, ROWS - 1):
         r = r0[i] - (g[i] * lift[i] - near(i, lift, cx, cy, cz))
@@ -611,26 +643,28 @@
         *fields_i, edge, resid_i,
     )
     one_x, two_x = swap(first, "coarse", False), swap(second, "coarse", True)
-    first, second = call(pack_third, [(23, 8, 128)] * 2, ins=[SMEM] + [VMEM] * 5)(
-        flags, resid_i, resid_o, packed, one_x, two_x
+    first, second = call(pack_own, [(13, 8, 128)] * 2, ins=[SMEM] + [VMEM] * 3)(
+        flags, resid_i, resid_o, packed
     )
     one, two = swap(first, "fine", False), swap(second, "fine", True)
+    first, second = call(pack_halo, [(10, 8, 128)] * 2, ins=[SMEM] + [VMEM] * 2)(flags, one_x, two_x)
+    one_out, two_out = swap(first, "fine", False), swap(second, "fine", True)
     count = nx * ny
     basis, message = call(
         krylov,
         [(3, 6, 16, 128), (256, 128)],
         [pltpu.VMEM((5, 10, 16, 128), f32), pltpu.VMEM((10, 16, 128), f32)],
-        ins=[SMEM] + [VMEM] * 6,
-    )(flags, packed, weight, one_x, two_x, one, two)
+        ins=[SMEM] + [VMEM] * 8,
+    )(flags, packed, weight, one_x, two_x, one, two, one_out, two_out)
     gathered = lax.all_to_all(message[:count], ("coarse", "fine"), 0, 0, tiled=True)
     out, correction = call(
         finish,
         [block, (4, 4, 64)],
         [ring] * 4,
-        ins=[SMEM] + [VMEM] * 20,
+        ins=[SMEM] + [VMEM] * 22,
     )(
         flags, gathered, basis, *fields_i, *fields_o, resid_i, resid_o, iterate_i, iterate_o,
-        one_x, two_x, one, two,
+        one_x, two_x, one, two, one_out, two_out,
     )
     return (out, correction)
 

time: 66.6 us -> 66 us (level)
  waiting for transfers between devices: 9.28 us -> 5.3 us
  starting transfers between devices: 20.3 us -> 23.2 us
    ppermute x10 -> x12, waiting for transfers between devices: 9.28 us -> 5.3 us  [swap(): return lax.ppermute(values, axis, list(enumerate(other)))]
    ppermute x10 -> x12, starting transfers between devices: 20.3 us -> 23.2 us  [swap(): return lax.ppermute(values, axis, list(enumerate(other)))]
    pallas_call x2 -> x3, Pallas kernels: 3.55 us -> 4.1 us  [the longest x1 2.97 us: body(): call(finish, [block, (4, 4, 64)], [ring] * 4, ins=[SMEM] + [VMEM] * 22)]
  transfers between devices with their start and end apart: 10 -> 12, of which waited for: 5 -> 2; matrix products, arithmetic and copies ran while one was open for 0% -> 0% of each run, Pallas kernels for 6% -> 8%
where the time goes in v1:
time: 66 us; the launch traced here: 65.9 us
  blocking collectives  24 us (36%)
  starting transfers between devices  23.2 us (35%)
  Pallas kernels  12.5 us (19%)
  waiting for transfers between devices  5.3 us (8%)
  between operations  0.82 us (1%)
    all_to_all x1, blocking collectives, body(): lax.all_to_all(message[:count], ('coarse', 'fine'), 0, 0, tiled=True)  24 us
    ppermute x12, starting transfers between devices, swap(): return lax.ppermute(values, axis, list(enumerate(other)))  23.2 us
    ppermute x12, waiting for transfers between devices, swap(): return lax.ppermute(values, axis, list(enumerate(other)))  5.3 us
    pallas_call x1, Pallas kernels, body(): call(finish, [block, (4, 4, 64)], [ring] * 4, ins=[SMEM] + [VMEM] * 22)  2.97 us
    pallas_call x1, Pallas kernels, pack_first_call(): pl.pallas_call(pack_first, out_shape=[jax.ShapeDtypeStruct((16, SIDE, LON...  2.01 us
    pallas_call x1, Pallas kernels, body(): call(smooth_inner, [inner] * 5 + [(18, RING, LONG), (11, SIDE, LONG), (9,...  1.55 us
    pallas_call x1, Pallas kernels, body(): call(smooth_outer, [outer] * 5 + [(5, SIDE, LONG), (7, SIDE, LONG)] + [(5...  1.47 us
  transfers between devices with their start and end apart: 12, of which 2 were waited for; matrix products, arithmetic and copies ran while one was open for 0% of the time, Pallas kernels for 8%

profile of v1, /device:TPU:1, one launch (start us, length us, event | category | flops | bytes accessed | tf_op | source)
XLA Modules:
  0.0 65.9 jit_solution(15214209325111531503)
XLA Ops:
  0.6 0.0 copy-start
  0.6 0.0 copy-start.1
  0.7 0.0 copy-start.2
  0.7 0.0 copy-start.3
  0.7 0.0 copy-start.4
  0.7 2.0 %shard_map.77 = (f32[16,16,256]{2,1,0:T(8,128)}, f32[16,16,256]{2,1,0:T(8,128)}) custom-call(f32[16,16,256]{2,1,0:T(8,128)} %src.7, f32[16,16,256]{2,1,0:T(8,128)} %cx.9, f32[16,16,256]{2,1,0:T(8,128)} %cy.9, f32[16,16,256]{2,1,0:T(8,128)} %cz.9, f32[16,16,256]{2,1,0:T(8,128)} %ab.5), custom_call_target="tpu_custom_call" | custom-call | tf_op jit(solution)/shard_map/pallas_call | solution.py:85
  2.7 3.3 %collective-permute-start = (f32[16,16,256]{2,1,0:T(8,128)}, f32[16,16,256]{2,1,0:T(8,128)S(1)}, u32[]{:S(2)}, u32[]{:S(2)}) collective-permute-start(f32[16,16,256]{2,1,0:T(8,128)} %get-tuple-element.37), channel_id=1, source_target_pairs={{0,16},{16,0},{32,48},{48,32},{64,80},{80,64},{96,112},{112,96},{1... | collective-permute-start | bytes 786440 | tf_op jit(solution)/shard_map/ppermute | solution.py:609
  6.0 0.0 collective-permute-start.1
  6.0 0.1 stack.27
  6.1 0.0 copy-done
  6.1 0.0 copy-done.1
  6.1 0.0 copy-done.2
  6.1 0.0 copy-done.3
  6.2 0.0 copy-done.4
  6.2 0.8 %shard_map.80 = (f32[16,16,256]{2,1,0:T(8,128)S(1)}, f32[8,24,256]{2,1,0:T(8,128)S(1)}, f32[8,24,256]{2,1,0:T(8,128)S(1)}) custom-call(s32[6]{0:T(128)S(1)} %convert_element_type.3.flags, f32[16,16,256]{2,1,0:T(8,128)S(1)} %copy-done.3, f32[16,16,256]{2,1,0:T(8,128)S(1)} %copy-done, f32[16,16,256]{2,1,0:T(8,128)S(1)} %copy-done.1, ...), custom_call_target="tpu_custom_call" | custom-call | tf_op jit(solution)/shard_map/pallas_call | solution.py:621
  7.0 1.2 %collective-permute-start.4 = (f32[8,24,256]{2,1,0:T(8,128)S(1)}, f32[8,24,256]{2,1,0:T(8,128)S(1)}, u32[]{:S(2)}, u32[]{:S(2)}) collective-permute-start(f32[8,24,256]{2,1,0:T(8,128)S(1)} %get-tuple-element.45), channel_id=1, source_target_pairs={{0,1},{1,0},{2,3},{3,2},{4,5},{5,4},{6,7},{7,6},{8,9},{9,8},{10,11... | collective-permute-start | bytes 589832 | tf_op jit(solution)/shard_map/ppermute | solution.py:609
  8.1 4.3 %collective-permute-start.5 = (f32[8,24,256]{2,1,0:T(8,128)S(1)}, f32[8,24,256]{2,1,0:T(8,128)S(1)}, u32[]{:S(2)}, u32[]{:S(2)}) collective-permute-start(f32[8,24,256]{2,1,0:T(8,128)S(1)} %get-tuple-element.46), channel_id=1, source_target_pairs={{0,15},{1,2},{2,1},{3,4},{4,3},{5,6},{6,5},{7,8},{8,7},{9,10},{10,... | collective-permute-start | bytes 589832 | tf_op jit(solution)/shard_map/ppermute | solution.py:609
  12.4 0.0 collective-permute-done.one.one_x
  12.4 0.0 collective-permute-done.1.two.two_x
  12.4 0.7 %shard_map.78 = (f32[7,16,256]{2,1,0:T(8,128)S(1)}, f32[3,24,256]{2,1,0:T(8,128)S(1)}, f32[3,24,256]{2,1,0:T(8,128)S(1)}) custom-call(s32[6]{0:T(128)S(1)} %convert_element_type.3.flags, f32[16,16,256]{2,1,0:T(8,128)S(1)} %copy-done.3, f32[16,16,256]{2,1,0:T(8,128)S(1)} %copy-done, f32[16,16,256]{2,1,0:T(8,128)S(1)} %copy-done.1, ...), custom_call_target="tpu_custom_call" | custom-call | tf_op jit(solution)/shard_map/pallas_call | solution.py:625
  13.1 0.0 copy-start.5
  13.1 0.1 collective-permute-start.2
  13.2 3.3 %collective-permute-start.3 = (f32[3,24,256]{2,1,0:T(8,128)S(1)}, f32[3,24,256]{2,1,0:T(8,128)S(1)}, u32[]{:S(2)}, u32[]{:S(2)}) collective-permute-start(f32[3,24,256]{2,1,0:T(8,128)S(1)} %get-tuple-element.41), channel_id=1, source_target_pairs={{0,15},{1,2},{2,1},{3,4},{4,3},{5,6},{6,5},{7,8},{8,7},{9,10},{10,... | collective-permute-start | bytes 221192 | tf_op jit(solution)/shard_map/ppermute | solution.py:609
  16.5 0.0 copy-done.5
  16.6 0.9 %shard_map.79 = (f32[4,4,8,128]{3,2,1,0:T(8,128)S(1)}, f32[8,128]{1,0:T(8,128)S(1)}) custom-call(f32[16,16,256]{2,1,0:T(8,128)S(1)} %copy-done, f32[16,16,256]{2,1,0:T(8,128)S(1)} %copy-done.1, f32[16,16,256]{2,1,0:T(8,128)S(1)} %copy-done.2, f32[16,16,256]{2,1,0:T(8,128)S(1)} %copy-done.4, s32[1,1,16]{2,1,0:T(1,128)S(1)} %copy-done.5), custom_call_target="tpu_custom_call" | custom-call | tf_op jit(solution)/shard_map/pallas_call | solution.py:620
  17.5 0.0 collective-permute-done.4.one
  17.5 0.0 collective-permute-done.5.two
  17.5 1.5 %shard_map.81 = (f32[15,24,256]{2,1,0:T(8,128)S(1)}, f32[15,24,256]{2,1,0:T(8,128)S(1)}, f32[15,24,256]{2,1,0:T(8,128)S(1)}, f32[15,24,256]{2,1,0:T(8,128)S(1)},...) custom-call(s32[6]{0:T(128)S(1)} %convert_element_type.3.flags, ...), custom_call_target="tpu_custom_call" | custom-call | tf_op jit(solution)/shard_map/pallas_call | solution.py:630
  19.0 0.0 collective-permute-done.2.one
  19.1 1.8 %collective-permute-done.3.two = f32[3,24,256]{2,1,0:T(8,128)S(1)} collective-permute-done((f32[3,24,256]{2,1,0:T(8,128)S(1)}, f32[3,24,256]{2,1,0:T(8,128)S(1)}, u32[]{:S(2)}, u32[]{:S(2)}) %collective-permute-start.3) | collective-permute-done | bytes 73760 | tf_op jit(solution)/shard_map/ppermute | solution.py:609
  20.9 1.5 %shard_map.82 = (f32[7,24,256]{2,1,0:T(8,128)S(1)}, f32[7,24,256]{2,1,0:T(8,128)S(1)}, f32[7,24,256]{2,1,0:T(8,128)S(1)}, f32[7,24,256]{2,1,0:T(8,128)S(1)}, f32...) custom-call(s32[6]{0:T(128)S(1)} %convert_element_type.3.flags, ...), custom_call_target="tpu_custom_call" | custom-call | tf_op jit(solution)/shard_map/pallas_call | solution.py:636
  22.4 5.1 %collective-permute-start.6 = (f32[12,8,128]{2,1,0:T(8,128)S(1)}, f32[12,8,128]{2,1,0:T(8,128)S(1)}, u32[]{:S(2)}, u32[]{:S(2)}) collective-permute-start(f32[12,8,128]{2,1,0:T(8,128)S(1)} %get-tuple-element.56), channel_id=1, source_target_pairs={{0,16},{16,0},{32,48},{48,32},{64,80},{80,64},{96,112},{112,96},{1... | collective-permute-start | bytes 147464 | tf_op jit(solution)/shard_map/ppermute | solution.py:609
  27.4 0.0 collective-permute-start.7
  27.4 0.6 shard_map.83
  28.0 0.1 collective-permute-start.8
  28.1 2.9 %collective-permute-start.9 = (f32[13,8,128]{2,1,0:T(8,128)S(1)}, f32[13,8,128]{2,1,0:T(8,128)S(1)}, u32[]{:S(2)}, u32[]{:S(2)}) collective-permute-start(f32[13,8,128]{2,1,0:T(8,128)S(1)} %get-tuple-element.60), channel_id=1, source_target_pairs={{0,15},{1,2},{2,1},{3,4},{4,3},{5,6},{6,5},{7,8},{8,7},{9,10},{10,... | collective-permute-start | bytes 159752 | tf_op jit(solution)/shard_map/ppermute | solution.py:609
  31.1 0.0 collective-permute-done.6.one_x
  31.1 0.0 collective-permute-done.7.two_x
  31.1 0.6 shard_map.84
  31.6 0.1 collective-permute-start.10
  31.7 2.8 %collective-permute-start.11 = (f32[10,8,128]{2,1,0:T(8,128)S(1)}, f32[10,8,128]{2,1,0:T(8,128)S(1)}, u32[]{:S(2)}, u32[]{:S(2)}) collective-permute-start(f32[10,8,128]{2,1,0:T(8,128)S(1)} %get-tuple-element.62), channel_id=1, source_target_pairs={{0,15},{1,2},{2,1},{3,4},{4,3},{5,6},{6,5},{7,8},{8,7},{9,10},{10,... | collective-permute-start | bytes 122888 | tf_op jit(solution)/shard_map/ppermute | solution.py:609
  34.6 0.0 collective-permute-done.8.one
  34.6 0.0 collective-permute-done.9.two
  34.6 0.0 collective-permute-done.10.one_out
  34.6 3.4 %collective-permute-done.11.two_out = f32[10,8,128]{2,1,0:T(8,128)S(1)} collective-permute-done((f32[10,8,128]{2,1,0:T(8,128)S(1)}, f32[10,8,128]{2,1,0:T(8,128)S(1)}, u32[]{:S(2)}, u32[]{:S(2)}) %collective-permute-start.11) | collective-permute-done | bytes 40992 | tf_op jit(solution)/shard_map/ppermute | solution.py:609
  38.0 1.0 %shard_map.85 = (f32[3,6,16,128]{3,2,1,0:T(8,128)S(1)}, f32[256,128]{1,0:T(8,128)S(1)}) custom-call(s32[6]{0:T(128)S(1)} %convert_element_type.3.flags, f32[5,8,128]{2,1,0:T(8,128)S(1)} %get-tuple-element.54.packed, f32[4,8,128]{2,1,0:T(8,128)S(1)} %get-tuple-element.55.weight, f32[12,8,128]{2,1,0:T(8,128)S(1)} %collective-permute-done.6.one_x, ...), custom_call_target="tpu_custom_call" | custom-call | tf_op jit(solution)/shard_map/pallas_call | solution.py:653
  39.0 24.0 %all_to_all.11 = f32[256,1,128]{2,1,0:T(1,128)S(1)} all-to-all(f32[256,1,128]{2,1,0:T(1,128)S(1)} %bitcast.11), channel_id=1, replica_groups=mesh['coarse'=16,'fine'=16] {'coarse','fine'}, dimensions={0} | all-to-all | bytes 262144 | tf_op jit(solution)/shard_map/all_to_all | solution.py:659
  62.9 3.0 %shard_map.86 = (f32[16,16,256]{2,1,0:T(8,128)}, f32[4,4,64]{2,1,0:T(4,128)}) custom-call(s32[6]{0:T(128)S(1)} %convert_element_type.3.flags, f32[256,128]{1,0:T(8,128)S(1)} %bitcast.10, f32[3,6,16,128]{3,2,1,0:T(8,128)S(1)} %get-tuple-element.64.basis, f32[15,24,256]{2,1,0:T(8,128)S(1)} %get-tuple-element.47.cx_i, ...), custom_call_target="tpu_custom_call" | custom-call | tf_op jit(solution)/shard_map/pallas_call | solution.py:660
  (1 shorter events, 0.0 us)
Async XLA Ops:
  0.6 5.5 %copy-start = (f32[16,16,256]{2,1,0:T(8,128)S(1)}, f32[16,16,256]{2,1,0:T(8,128)}, u32[]{:S(2)}) copy-start(f32[16,16,256]{2,1,0:T(8,128)} %cx.9) | copy-start | bytes 786436
  0.6 5.5 %copy-start.1 = (f32[16,16,256]{2,1,0:T(8,128)S(1)}, f32[16,16,256]{2,1,0:T(8,128)}, u32[]{:S(2)}) copy-start(f32[16,16,256]{2,1,0:T(8,128)} %cy.9) | copy-start | bytes 786436
  0.7 5.5 %copy-start.2 = (f32[16,16,256]{2,1,0:T(8,128)S(1)}, f32[16,16,256]{2,1,0:T(8,128)}, u32[]{:S(2)}) copy-start(f32[16,16,256]{2,1,0:T(8,128)} %cz.9) | copy-start | bytes 786436
  0.7 5.5 %copy-start.3 = (f32[16,16,256]{2,1,0:T(8,128)S(1)}, f32[16,16,256]{2,1,0:T(8,128)}, u32[]{:S(2)}) copy-start(f32[16,16,256]{2,1,0:T(8,128)} %src.7) | copy-start | bytes 786436
  0.7 5.5 %copy-start.4 = (f32[16,16,256]{2,1,0:T(8,128)S(1)}, f32[16,16,256]{2,1,0:T(8,128)}, u32[]{:S(2)}) copy-start(f32[16,16,256]{2,1,0:T(8,128)} %ab.5) | copy-start | bytes 786436
  2.7 9.7 %collective-permute-start = (f32[16,16,256]{2,1,0:T(8,128)}, f32[16,16,256]{2,1,0:T(8,128)S(1)}, u32[]{:S(2)}, u32[]{:S(2)}) collective-permute-start(f32[16,16,256]{2,1,0:T(8,128)} %get-tuple-element.37), channel_id=1, source_target_pairs={{0,16},{16,0},{32,48},{48,32},{64,80},{80,64},{96,112},{112,96},{1... | collective-permute-start | bytes 786440 | tf_op jit(solution)/shard_map/ppermute | solution.py:609
  6.0 6.4 %collective-permute-start.1 = (f32[16,16,256]{2,1,0:T(8,128)}, f32[16,16,256]{2,1,0:T(8,128)S(1)}, u32[]{:S(2)}, u32[]{:S(2)}) collective-permute-start(f32[16,16,256]{2,1,0:T(8,128)} %get-tuple-element.38), channel_id=1, source_target_pairs={{0,240},{16,32},{32,16},{48,64},{64,48},{80,96},{96,80},{112,128},... | collective-permute-start | bytes 786440 | tf_op jit(solution)/shard_map/ppermute | solution.py:609
  7.0 10.5 %collective-permute-start.4 = (f32[8,24,256]{2,1,0:T(8,128)S(1)}, f32[8,24,256]{2,1,0:T(8,128)S(1)}, u32[]{:S(2)}, u32[]{:S(2)}) collective-permute-start(f32[8,24,256]{2,1,0:T(8,128)S(1)} %get-tuple-element.45), channel_id=1, source_target_pairs={{0,1},{1,0},{2,3},{3,2},{4,5},{5,4},{6,7},{7,6},{8,9},{9,8},{10,11... | collective-permute-start | bytes 589832 | tf_op jit(solution)/shard_map/ppermute | solution.py:609
  8.1 9.3 %collective-permute-start.5 = (f32[8,24,256]{2,1,0:T(8,128)S(1)}, f32[8,24,256]{2,1,0:T(8,128)S(1)}, u32[]{:S(2)}, u32[]{:S(2)}) collective-permute-start(f32[8,24,256]{2,1,0:T(8,128)S(1)} %get-tuple-element.46), channel_id=1, source_target_pairs={{0,15},{1,2},{2,1},{3,4},{4,3},{5,6},{6,5},{7,8},{8,7},{9,10},{10,... | collective-permute-start | bytes 589832 | tf_op jit(solution)/shard_map/ppermute | solution.py:609
  13.1 3.5 %copy-start.5 = (s32[1,1,16]{2,1,0:T(1,128)S(1)}, s32[1,1,16]{2,1,0:T(1,128)}, u32[]{:S(2)}) copy-start(s32[1,1,16]{2,1,0:T(1,128)} %active.1) | copy-start | bytes 196
  13.1 5.9 %collective-permute-start.2 = (f32[3,24,256]{2,1,0:T(8,128)S(1)}, f32[3,24,256]{2,1,0:T(8,128)S(1)}, u32[]{:S(2)}, u32[]{:S(2)}) collective-permute-start(f32[3,24,256]{2,1,0:T(8,128)S(1)} %get-tuple-element.40), channel_id=1, source_target_pairs={{0,1},{1,0},{2,3},{3,2},{4,5},{5,4},{6,7},{7,6},{8,9},{9,8},{10,11... | collective-permute-start | bytes 221192 | tf_op jit(solution)/shard_map/ppermute | solution.py:609
  13.2 7.7 %collective-permute-start.3 = (f32[3,24,256]{2,1,0:T(8,128)S(1)}, f32[3,24,256]{2,1,0:T(8,128)S(1)}, u32[]{:S(2)}, u32[]{:S(2)}) collective-permute-start(f32[3,24,256]{2,1,0:T(8,128)S(1)} %get-tuple-element.41), channel_id=1, source_target_pairs={{0,15},{1,2},{2,1},{3,4},{4,3},{5,6},{6,5},{7,8},{8,7},{9,10},{10,... | collective-permute-start | bytes 221192 | tf_op jit(solution)/shard_map/ppermute | solution.py:609
  22.4 8.7 %collective-permute-start.6 = (f32[12,8,128]{2,1,0:T(8,128)S(1)}, f32[12,8,128]{2,1,0:T(8,128)S(1)}, u32[]{:S(2)}, u32[]{:S(2)}) collective-permute-start(f32[12,8,128]{2,1,0:T(8,128)S(1)} %get-tuple-element.56), channel_id=1, source_target_pairs={{0,16},{16,0},{32,48},{48,32},{64,80},{80,64},{96,112},{112,96},{1... | collective-permute-start | bytes 147464 | tf_op jit(solution)/shard_map/ppermute | solution.py:609
  27.4 3.6 %collective-permute-start.7 = (f32[12,8,128]{2,1,0:T(8,128)S(1)}, f32[12,8,128]{2,1,0:T(8,128)S(1)}, u32[]{:S(2)}, u32[]{:S(2)}) collective-permute-start(f32[12,8,128]{2,1,0:T(8,128)S(1)} %get-tuple-element.57), channel_id=1, source_target_pairs={{0,240},{16,32},{32,16},{48,64},{64,48},{80,96},{96,80},{112,128},... | collective-permute-start | bytes 147464 | tf_op jit(solution)/shard_map/ppermute | solution.py:609
  28.0 6.6 %collective-permute-start.8 = (f32[13,8,128]{2,1,0:T(8,128)S(1)}, f32[13,8,128]{2,1,0:T(8,128)S(1)}, u32[]{:S(2)}, u32[]{:S(2)}) collective-permute-start(f32[13,8,128]{2,1,0:T(8,128)S(1)} %get-tuple-element.59), channel_id=1, source_target_pairs={{0,1},{1,0},{2,3},{3,2},{4,5},{5,4},{6,7},{7,6},{8,9},{9,8},{10,11... | collective-permute-start | bytes 159752 | tf_op jit(solution)/shard_map/ppermute | solution.py:609
  28.1 6.5 %collective-permute-start.9 = (f32[13,8,128]{2,1,0:T(8,128)S(1)}, f32[13,8,128]{2,1,0:T(8,128)S(1)}, u32[]{:S(2)}, u32[]{:S(2)}) collective-permute-start(f32[13,8,128]{2,1,0:T(8,128)S(1)} %get-tuple-element.60), channel_id=1, source_target_pairs={{0,15},{1,2},{2,1},{3,4},{4,3},{5,6},{6,5},{7,8},{8,7},{9,10},{10,... | collective-permute-start | bytes 159752 | tf_op jit(solution)/shard_map/ppermute | solution.py:609
  31.6 2.9 %collective-permute-start.10 = (f32[10,8,128]{2,1,0:T(8,128)S(1)}, f32[10,8,128]{2,1,0:T(8,128)S(1)}, u32[]{:S(2)}, u32[]{:S(2)}) collective-permute-start(f32[10,8,128]{2,1,0:T(8,128)S(1)} %get-tuple-element.61), channel_id=1, source_target_pairs={{0,1},{1,0},{2,3},{3,2},{4,5},{5,4},{6,7},{7,6},{8,9},{9,8},{10,11... | collective-permute-start | bytes 122888 | tf_op jit(solution)/shard_map/ppermute | solution.py:609
  31.7 6.3 %collective-permute-start.11 = (f32[10,8,128]{2,1,0:T(8,128)S(1)}, f32[10,8,128]{2,1,0:T(8,128)S(1)}, u32[]{:S(2)}, u32[]{:S(2)}) collective-permute-start(f32[10,8,128]{2,1,0:T(8,128)S(1)} %get-tuple-element.62), channel_id=1, source_target_pairs={{0,15},{1,2},{2,1},{3,4},{4,3},{5,6},{6,5},{7,8},{8,7},{9,10},{10,... | collective-permute-start | bytes 122888 | tf_op jit(solution)/shard_map/ppermute | solution.py:609

commit v2 on v1

--- a/solution.py
+++ b/solution.py
@@ -15,7 +15,6 @@
 ROWS = SIDE + 6
 RING = 24
 VMEM = pl.BlockSpec(memory_space=pltpu.VMEM)
-SMEM = pl.BlockSpec(memory_space=pltpu.SMEM)
 LIMIT = 24 * 1024 * 1024
 
 
@@ -53,6 +52,12 @@
         scratch_shapes=list(scratch),
         compiler_params=pltpu.CompilerParams(vmem_limit_bytes=LIMIT),
     )
+
+
+def place():
+    ix, iy = lax.axis_index("coarse"), lax.axis_index("fine")
+    nx, ny = lax.axis_size("coarse"), lax.axis_size("fine")
+    return ix, nx - 1 - ix, iy, ny - 1 - iy, 1 - iy % 2, 1 - ix % 2
 
 
 def pack_first(*refs):
@@ -162,7 +167,8 @@
     return top, bottom
 
 
-def pack_inner(flags, src, cx, cy, cz, ab, diag, first, second):
+def pack_inner(src, cx, cy, cz, ab, diag, first, second):
+    flags = place()
     even = flags[4] > 0
     for x in range(1, SIDE):
         g = diagonal(cx[x], cx[x - 1], cy[x], cz[x], ab[x])
@@ -173,7 +179,8 @@
         second[at] = jnp.where(even, bottom, top)
 
 
-def pack_outer(flags, src, cx, cy, cz, ab, one, two, diag, first, second):
+def pack_outer(src, cx, cy, cz, ab, one, two, diag, first, second):
+    flags = place()
     even = flags[4] > 0
     has_low, has_high = flags[0] > 0, flags[1] > 0
     low, high = sides(one, two, flags[5] > 0, has_low, has_high)
@@ -279,9 +286,10 @@
 
 
 def smooth_inner(
-    flags, src, cx, cy, cz, diag, one, two,
+    src, cx, cy, cz, diag, one, two,
     cx_o, cy_o, cz_o, g_o, inv_o, edge, iterate, resid, u0, u1, u2, r,
 ):
+    flags = place()
     center, m1, q1, m2, q2 = FINE
     left, right = sides(one, two, flags[4] > 0, flags[2] > 0, flags[3] > 0)
     hit = inside_ring(flags)
@@ -313,10 +321,11 @@
 
 
 def smooth_outer(
-    flags, src, cx, cy, cz, one_x, two_x, diag, one, two, coarse, active,
+    src, cx, cy, cz, one_x, two_x, diag, one, two, coarse, active,
     cx_i, cy_i, cz_i, g_i, inv_i, edge, resid_i,
     cx_o, cy_o, cz_o, g_o, inv_o, iterate, resid, packed, weight, first, second,
 ):
+    flags = place()
     center, m1, q1, m2, q2 = FINE
     has_low, has_high = flags[0] > 0, flags[1] > 0
     low, high = sides(one_x, two_x, flags[5] > 0, has_low, has_high)
@@ -410,7 +419,8 @@
         second[at + c] = jnp.where(even, bottom, top)
 
 
-def pack_own(flags, resid_i, resid_o, packed, first, second):
+def pack_own(resid_i, resid_o, packed, first, second):
+    flags = place()
     def halves(x):
         mine = own_layer(x, resid_i, resid_o, 4, 12, 9)
         return [(mine[0:2, at : at + 128], mine[14:16, at : at + 128]) for at in (0, 128)]
@@ -422,7 +432,8 @@
         second[8 + k] = packed[k]
 
 
-def pack_halo(flags, one_x, two_x, first, second):
+def pack_halo(one_x, two_x, first, second):
+    flags = place()
     low, high = sides(one_x, two_x, flags[5] > 0, flags[0] > 0, flags[1] > 0)
 
     def halves(get, k):
@@ -438,7 +449,8 @@
             second[at] = tile
 
 
-def krylov(flags, packed, weight, one_x, two_x, one, two, one_out, two_out, basis, message, ext, t1s):
+def krylov(packed, weight, one_x, two_x, one, two, one_out, two_out, basis, message, ext, t1s):
+    flags = place()
     low, high = sides(one_x, two_x, flags[5] > 0, flags[0] > 0, flags[1] > 0)
     left, right = sides(one, two, flags[4] > 0, flags[2] > 0, flags[3] > 0)
     left_out, right_out = sides(one_out, two_out, flags[4] > 0, flags[2] > 0, flags[3] > 0)
@@ -515,10 +527,11 @@
 
 
 def finish(
-    flags, gathered, basis, cx_i, cy_i, cz_i, g_i, inv_i, cx_o, cy_o, cz_o, g_o, inv_o,
+    gathered, basis, cx_i, cy_i, cz_i, g_i, inv_i, cx_o, cy_o, cz_o, g_o, inv_o,
     resid_i, resid_o, iterate_i, iterate_o, one_x, two_x, one, two, one_out, two_out,
     out, correction, lift, u0, u1, r0,
 ):
+    flags = place()
     center, m1, q1, m2, q2 = FINE
     low, high = sides(one_x, two_x, flags[5] > 0, flags[0] > 0, flags[1] > 0)
     left, right = sides(one, two, flags[4] > 0, flags[2] > 0, flags[3] > 0)
@@ -610,60 +623,57 @@
 
 
 def body(src, cx, cy, cz, ab, active):
-    ix, iy = lax.axis_index("coarse"), lax.axis_index("fine")
-    nx, ny = lax.axis_size("coarse"), lax.axis_size("fine")
-    flags = jnp.stack([ix > 0, ix < nx - 1, iy > 0, iy < ny - 1, iy % 2 == 0, ix % 2 == 0]).astype(jnp.int32)
+    count = lax.axis_size("coarse") * lax.axis_size("fine")
     block, ring = (SIDE, SIDE, LONG), pltpu.VMEM((ROWS, RING, LONG), f32)
 
     first, second = pack_first_call((src, cx, cy, cz, ab))
     one_x, two_x = swap(first, "coarse", False), swap(second, "coarse", True)
     coarse, mask = call(coarsen, [(4, 4, 8, 128), (8, 128)], ins=[VMEM] * 5)(cx, cy, cz, ab, active)
     diag, first, second = call(
-        pack_inner, [block, (8, 24, LONG), (8, 24, LONG)], ins=[SMEM] + [VMEM] * 5
-    )(flags, src, cx, cy, cz, ab)
+        pack_inner, [block, (8, 24, LONG), (8, 24, LONG)], ins=[VMEM] * 5
+    )(src, cx, cy, cz, ab)
     one, two = swap(first, "fine", False), swap(second, "fine", True)
     diag_out, first, second = call(
-        pack_outer, [(7, SIDE, LONG), (3, 24, LONG), (3, 24, LONG)], ins=[SMEM] + [VMEM] * 7
-    )(flags, src, cx, cy, cz, ab, one_x, two_x)
+        pack_outer, [(7, SIDE, LONG), (3, 24, LONG), (3, 24, LONG)], ins=[VMEM] * 7
+    )(src, cx, cy, cz, ab, one_x, two_x)
     one_out, two_out = swap(first, "fine", False), swap(second, "fine", True)
     inner, outer = (15, RING, LONG), (7, RING, LONG)
     *fields_i, edge, iterate_i, resid_i = call(
         smooth_inner,
         [inner] * 5 + [(18, RING, LONG), (11, SIDE, LONG), (9, SIDE, LONG)],
         [pltpu.VMEM(inner, f32)] * 4,
-        ins=[SMEM] + [VMEM] * 7,
-    )(flags, src, cx, cy, cz, diag, one, two)
+        ins=[VMEM] * 7,
+    )(src, cx, cy, cz, diag, one, two)
     *fields_o, iterate_o, resid_o, packed, weight, first, second = call(
         smooth_outer,
         [outer] * 5 + [(5, SIDE, LONG), (7, SIDE, LONG)]
         + [(5, 8, 128), (4, 8, 128), (12, 8, 128), (12, 8, 128)],
-        ins=[SMEM] + [VMEM] * 18,
+        ins=[VMEM] * 18,
     )(
-        flags, src, cx, cy, cz, one_x, two_x, diag_out, one_out, two_out, coarse, mask,
+        src, cx, cy, cz, one_x, two_x, diag_out, one_out, two_out, coarse, mask,
         *fields_i, edge, resid_i,
     )
     one_x, two_x = swap(first, "coarse", False), swap(second, "coarse", True)
-    first, second = call(pack_own, [(13, 8, 128)] * 2, ins=[SMEM] + [VMEM] * 3)(
-        flags, resid_i, resid_o, packed
+    first, second = call(pack_own, [(13, 8, 128)] * 2, ins=[VMEM] * 3)(
+        resid_i, resid_o, packed
     )
     one, two = swap(first, "fine", False), swap(second, "fine", True)
-    first, second = call(pack_halo, [(10, 8, 128)] * 2, ins=[SMEM] + [VMEM] * 2)(flags, one_x, two_x)
+    first, second = call(pack_halo, [(10, 8, 128)] * 2, ins=[VMEM] * 2)(one_x, two_x)
     one_out, two_out = swap(first, "fine", False), swap(second, "fine", True)
-    count = nx * ny
     basis, message = call(
         krylov,
         [(3, 6, 16, 128), (256, 128)],
         [pltpu.VMEM((5, 10, 16, 128), f32), pltpu.VMEM((10, 16, 128), f32)],
-        ins=[SMEM] + [VMEM] * 8,
-    )(flags, packed, weight, one_x, two_x, one, two, one_out, two_out)
+        ins=[VMEM] * 8,
+    )(packed, weight, one_x, two_x, one, two, one_out, two_out)
     gathered = lax.all_to_all(message[:count], ("coarse", "fine"), 0, 0, tiled=True)
     out, correction = call(
         finish,
         [block, (4, 4, 64)],
         [ring] * 4,
-        ins=[SMEM] + [VMEM] * 22,
+        ins=[VMEM] * 22,
     )(
-        flags, gathered, basis, *fields_i, *fields_o, resid_i, resid_o, iterate_i, iterate_o,
+        gathered, basis, *fields_i, *fields_o, resid_i, resid_o, iterate_i, iterate_o,
         one_x, two_x, one, two, one_out, two_out,
     )
     return (out, correction)

time: 66 us -> 63.3 us (0.959)
  Pallas kernels: 12.5 us -> 8.18 us
  starting transfers between devices: 23.2 us -> 23.9 us
    pallas_call x5, Pallas kernels: 5.56 us -> 2.84 us  [the longest x1 2.4 us: body(): call(finish, [block, (4, 4, 64)], [ring] * 4, ins=[VMEM] * 22)]
    ppermute x12, starting transfers between devices: 23.2 us -> 23.9 us  [swap(): return lax.ppermute(values, axis, list(enumerate(other)))]
  transfers between devices with their start and end apart: 12 -> 12, of which waited for: 2 -> 3; matrix products, arithmetic and copies ran while one was open for 0% -> 0% of each run, Pallas kernels for 8% -> 4%
where the time goes in v2:
time: 63.3 us; the launch traced here: 63.2 us
  blocking collectives  24.5 us (39%)
  starting transfers between devices  23.9 us (38%)
  Pallas kernels  8.18 us (13%)
  waiting for transfers between devices  5.78 us (9%)
  between operations  0.81 us (1%)
    all_to_all x1, blocking collectives, body(): lax.all_to_all(message[:count], ('coarse', 'fine'), 0, 0, tiled=True)  24.5 us
    ppermute x12, starting transfers between devices, swap(): return lax.ppermute(values, axis, list(enumerate(other)))  23.9 us
    ppermute x12, waiting for transfers between devices, swap(): return lax.ppermute(values, axis, list(enumerate(other)))  5.78 us
    pallas_call x1, Pallas kernels, body(): call(finish, [block, (4, 4, 64)], [ring] * 4, ins=[VMEM] * 22)  2.4 us
    pallas_call x1, Pallas kernels, pack_first_call(): pl.pallas_call(pack_first, out_shape=[jax.ShapeDtypeStruct((16, SIDE, LON...  2.01 us
  transfers between devices with their start and end apart: 12, of which 3 were waited for; matrix products, arithmetic and copies ran while one was open for 0% of the time, Pallas kernels for 4%

profile of v2, /device:TPU:1, one launch (start us, length us, event | category | flops | bytes accessed | tf_op | source)
XLA Modules:
  0.0 63.2 jit_solution(1701630247573032808)
XLA Ops:
  0.6 0.0 copy-start.2
  0.6 0.0 copy-start.1
  0.7 0.0 copy-start
  0.7 0.0 copy-start.3
  0.7 0.0 copy-start.4
  0.7 2.0 %shard_map.77 = (f32[16,16,256]{2,1,0:T(8,128)}, f32[16,16,256]{2,1,0:T(8,128)}) custom-call(f32[16,16,256]{2,1,0:T(8,128)} %src.7, f32[16,16,256]{2,1,0:T(8,128)} %cx.9, f32[16,16,256]{2,1,0:T(8,128)} %cy.9, f32[16,16,256]{2,1,0:T(8,128)} %cz.9, f32[16,16,256]{2,1,0:T(8,128)} %ab.5), custom_call_target="tpu_custom_call" | custom-call | tf_op jit(solution)/shard_map/pallas_call | solution.py:90
  2.7 3.3 %collective-permute-start = (f32[16,16,256]{2,1,0:T(8,128)}, f32[16,16,256]{2,1,0:T(8,128)S(1)}, u32[]{:S(2)}, u32[]{:S(2)}) collective-permute-start(f32[16,16,256]{2,1,0:T(8,128)} %get-tuple-element.37), channel_id=1, source_target_pairs={{0,16},{16,0},{32,48},{48,32},{64,80},{80,64},{96,112},{112,96},{1... | collective-permute-start | bytes 786440 | tf_op jit(solution)/shard_map/ppermute | solution.py:622
  6.0 0.0 collective-permute-start.1
  6.0 0.0 copy-done.2
  6.0 0.0 copy-done.1
  6.0 0.0 copy-done
  6.0 0.0 copy-done.3
  6.0 0.0 copy-done.4
  6.1 0.2 shard_map.80
  6.3 1.2 %collective-permute-start.4 = (f32[8,24,256]{2,1,0:T(8,128)S(1)}, f32[8,24,256]{2,1,0:T(8,128)S(1)}, u32[]{:S(2)}, u32[]{:S(2)}) collective-permute-start(f32[8,24,256]{2,1,0:T(8,128)S(1)} %get-tuple-element.45), channel_id=1, source_target_pairs={{0,1},{1,0},{2,3},{3,2},{4,5},{5,4},{6,7},{7,6},{8,9},{9,8},{10,11... | collective-permute-start | bytes 589832 | tf_op jit(solution)/shard_map/ppermute | solution.py:622
  7.5 4.3 %collective-permute-start.5 = (f32[8,24,256]{2,1,0:T(8,128)S(1)}, f32[8,24,256]{2,1,0:T(8,128)S(1)}, u32[]{:S(2)}, u32[]{:S(2)}) collective-permute-start(f32[8,24,256]{2,1,0:T(8,128)S(1)} %get-tuple-element.46), channel_id=1, source_target_pairs={{0,15},{1,2},{2,1},{3,4},{4,3},{5,6},{6,5},{7,8},{8,7},{9,10},{10,... | collective-permute-start | bytes 589832 | tf_op jit(solution)/shard_map/ppermute | solution.py:622
  11.7 0.0 collective-permute-done.one.one_x
  11.7 0.6 collective-permute-done.1.two.two_x
  12.3 0.1 shard_map.78
  12.5 0.0 copy-start.5
  12.5 0.1 collective-permute-start.2
  12.6 3.4 %collective-permute-start.3 = (f32[3,24,256]{2,1,0:T(8,128)S(1)}, f32[3,24,256]{2,1,0:T(8,128)S(1)}, u32[]{:S(2)}, u32[]{:S(2)}) collective-permute-start(f32[3,24,256]{2,1,0:T(8,128)S(1)} %get-tuple-element.41), channel_id=1, source_target_pairs={{0,15},{1,2},{2,1},{3,4},{4,3},{5,6},{6,5},{7,8},{8,7},{9,10},{10,... | collective-permute-start | bytes 221192 | tf_op jit(solution)/shard_map/ppermute | solution.py:622
  16.0 0.0 copy-done.5
  16.0 0.9 %shard_map.79 = (f32[4,4,8,128]{3,2,1,0:T(8,128)S(1)}, f32[8,128]{1,0:T(8,128)S(1)}) custom-call(f32[16,16,256]{2,1,0:T(8,128)S(1)} %copy-done, f32[16,16,256]{2,1,0:T(8,128)S(1)} %copy-done.1, f32[16,16,256]{2,1,0:T(8,128)S(1)} %copy-done.2, f32[16,16,256]{2,1,0:T(8,128)S(1)} %copy-done.4, s32[1,1,16]{2,1,0:T(1,128)S(1)} %copy-done.5), custom_call_target="tpu_custom_call" | custom-call | tf_op jit(solution)/shard_map/pallas_call | solution.py:631
  16.9 0.0 collective-permute-done.4.one
  16.9 0.0 collective-permute-done.5.two
  17.0 1.0 %shard_map.81 = (f32[15,24,256]{2,1,0:T(8,128)S(1)}, f32[15,24,256]{2,1,0:T(8,128)S(1)}, f32[15,24,256]{2,1,0:T(8,128)S(1)}, f32[15,24,256]{2,1,0:T(8,128)S(1)},...) custom-call(f32[16,16,256]{2,1,0:T(8,128)S(1)} %copy-done.3, ...), custom_call_target="tpu_custom_call" | custom-call | tf_op jit(solution)/shard_map/pallas_call | solution.py:641
  18.0 0.0 collective-permute-done.2.one
  18.0 2.3 %collective-permute-done.3.two = f32[3,24,256]{2,1,0:T(8,128)S(1)} collective-permute-done((f32[3,24,256]{2,1,0:T(8,128)S(1)}, f32[3,24,256]{2,1,0:T(8,128)S(1)}, u32[]{:S(2)}, u32[]{:S(2)}) %collective-permute-start.3) | collective-permute-done | bytes 73760 | tf_op jit(solution)/shard_map/ppermute | solution.py:622
  20.3 1.0 %shard_map.82 = (f32[7,24,256]{2,1,0:T(8,128)S(1)}, f32[7,24,256]{2,1,0:T(8,128)S(1)}, f32[7,24,256]{2,1,0:T(8,128)S(1)}, f32[7,24,256]{2,1,0:T(8,128)S(1)}, f32...) custom-call(f32[16,16,256]{2,1,0:T(8,128)S(1)} %copy-done.3, ...), custom_call_target="tpu_custom_call" | custom-call | tf_op jit(solution)/shard_map/pallas_call | solution.py:647
  21.3 4.5 %collective-permute-start.6 = (f32[12,8,128]{2,1,0:T(8,128)S(1)}, f32[12,8,128]{2,1,0:T(8,128)S(1)}, u32[]{:S(2)}, u32[]{:S(2)}) collective-permute-start(f32[12,8,128]{2,1,0:T(8,128)S(1)} %get-tuple-element.56), channel_id=1, source_target_pairs={{0,16},{16,0},{32,48},{48,32},{64,80},{80,64},{96,112},{112,96},{1... | collective-permute-start | bytes 147464 | tf_op jit(solution)/shard_map/ppermute | solution.py:622
  25.8 0.0 collective-permute-start.7
  25.8 0.1 collective-permute-start.8
  25.9 3.6 %collective-permute-start.9 = (f32[13,8,128]{2,1,0:T(8,128)S(1)}, f32[13,8,128]{2,1,0:T(8,128)S(1)}, u32[]{:S(2)}, u32[]{:S(2)}) collective-permute-start(f32[13,8,128]{2,1,0:T(8,128)S(1)} %get-tuple-element.60), channel_id=1, source_target_pairs={{0,15},{1,2},{2,1},{3,4},{4,3},{5,6},{6,5},{7,8},{8,7},{9,10},{10,... | collective-permute-start | bytes 159752 | tf_op jit(solution)/shard_map/ppermute | solution.py:622
  29.5 0.0 collective-permute-done.6.one_x
  29.5 0.0 collective-permute-done.7.two_x
  29.5 0.1 collective-permute-start.10
  29.6 3.4 %collective-permute-start.11 = (f32[10,8,128]{2,1,0:T(8,128)S(1)}, f32[10,8,128]{2,1,0:T(8,128)S(1)}, u32[]{:S(2)}, u32[]{:S(2)}) collective-permute-start(f32[10,8,128]{2,1,0:T(8,128)S(1)} %get-tuple-element.62), channel_id=1, source_target_pairs={{0,15},{1,2},{2,1},{3,4},{4,3},{5,6},{6,5},{7,8},{8,7},{9,10},{10,... | collective-permute-start | bytes 122888 | tf_op jit(solution)/shard_map/ppermute | solution.py:622
  33.0 0.0 collective-permute-done.8.one
  33.0 0.0 collective-permute-done.9.two
  33.0 0.0 collective-permute-done.10.one_out
  33.0 2.9 %collective-permute-done.11.two_out = f32[10,8,128]{2,1,0:T(8,128)S(1)} collective-permute-done((f32[10,8,128]{2,1,0:T(8,128)S(1)}, f32[10,8,128]{2,1,0:T(8,128)S(1)}, u32[]{:S(2)}, u32[]{:S(2)}) %collective-permute-start.11) | collective-permute-done | bytes 40992 | tf_op jit(solution)/shard_map/ppermute | solution.py:622
  35.9 0.4 shard_map.85
  36.3 24.5 %all_to_all.11 = f32[256,1,128]{2,1,0:T(1,128)S(1)} all-to-all(f32[256,1,128]{2,1,0:T(1,128)S(1)} %bitcast.5), channel_id=1, replica_groups=mesh['coarse'=16,'fine'=16] {'coarse','fine'}, dimensions={0} | all-to-all | bytes 262144 | tf_op jit(solution)/shard_map/all_to_all | solution.py:669
  60.8 2.4 %shard_map.86 = (f32[16,16,256]{2,1,0:T(8,128)}, f32[4,4,64]{2,1,0:T(4,128)}) custom-call(f32[256,128]{1,0:T(8,128)S(1)} %bitcast.4, f32[3,6,16,128]{3,2,1,0:T(8,128)S(1)} %get-tuple-element.64.basis, f32[15,24,256]{2,1,0:T(8,128)S(1)} %get-tuple-element.47.cx_i, f32[15,24,256]{2,1,0:T(8,128)S(1)} %get-tuple-element.48.cy_i, ...), custom_call_target="tpu_custom_call" | custom-call | tf_op jit(solution)/shard_map/pallas_call | solution.py:670
  (2 shorter events, 0.1 us)
Async XLA Ops:
  0.6 5.4 %copy-start.2 = (f32[16,16,256]{2,1,0:T(8,128)S(1)}, f32[16,16,256]{2,1,0:T(8,128)}, u32[]{:S(2)}) copy-start(f32[16,16,256]{2,1,0:T(8,128)} %cz.9) | copy-start | bytes 786436
  0.6 5.4 %copy-start.1 = (f32[16,16,256]{2,1,0:T(8,128)S(1)}, f32[16,16,256]{2,1,0:T(8,128)}, u32[]{:S(2)}) copy-start(f32[16,16,256]{2,1,0:T(8,128)} %cy.9) | copy-start | bytes 786436
  0.7 5.4 %copy-start = (f32[16,16,256]{2,1,0:T(8,128)S(1)}, f32[16,16,256]{2,1,0:T(8,128)}, u32[]{:S(2)}) copy-start(f32[16,16,256]{2,1,0:T(8,128)} %cx.9) | copy-start | bytes 786436
  0.7 5.4 %copy-start.3 = (f32[16,16,256]{2,1,0:T(8,128)S(1)}, f32[16,16,256]{2,1,0:T(8,128)}, u32[]{:S(2)}) copy-start(f32[16,16,256]{2,1,0:T(8,128)} %src.7) | copy-start | bytes 786436
  0.7 5.4 %copy-start.4 = (f32[16,16,256]{2,1,0:T(8,128)S(1)}, f32[16,16,256]{2,1,0:T(8,128)}, u32[]{:S(2)}) copy-start(f32[16,16,256]{2,1,0:T(8,128)} %ab.5) | copy-start | bytes 786436
  2.7 9.0 %collective-permute-start = (f32[16,16,256]{2,1,0:T(8,128)}, f32[16,16,256]{2,1,0:T(8,128)S(1)}, u32[]{:S(2)}, u32[]{:S(2)}) collective-permute-start(f32[16,16,256]{2,1,0:T(8,128)} %get-tuple-element.37), channel_id=1, source_target_pairs={{0,16},{16,0},{32,48},{48,32},{64,80},{80,64},{96,112},{112,96},{1... | collective-permute-start | bytes 786440 | tf_op jit(solution)/shard_map/ppermute | solution.py:622
  6.0 6.3 %collective-permute-start.1 = (f32[16,16,256]{2,1,0:T(8,128)}, f32[16,16,256]{2,1,0:T(8,128)S(1)}, u32[]{:S(2)}, u32[]{:S(2)}) collective-permute-start(f32[16,16,256]{2,1,0:T(8,128)} %get-tuple-element.38), channel_id=1, source_target_pairs={{0,240},{16,32},{32,16},{48,64},{64,48},{80,96},{96,80},{112,128},... | collective-permute-start | bytes 786440 | tf_op jit(solution)/shard_map/ppermute | solution.py:622
  6.3 10.6 %collective-permute-start.4 = (f32[8,24,256]{2,1,0:T(8,128)S(1)}, f32[8,24,256]{2,1,0:T(8,128)S(1)}, u32[]{:S(2)}, u32[]{:S(2)}) collective-permute-start(f32[8,24,256]{2,1,0:T(8,128)S(1)} %get-tuple-element.45), channel_id=1, source_target_pairs={{0,1},{1,0},{2,3},{3,2},{4,5},{5,4},{6,7},{7,6},{8,9},{9,8},{10,11... | collective-permute-start | bytes 589832 | tf_op jit(solution)/shard_map/ppermute | solution.py:622
  7.5 9.5 %collective-permute-start.5 = (f32[8,24,256]{2,1,0:T(8,128)S(1)}, f32[8,24,256]{2,1,0:T(8,128)S(1)}, u32[]{:S(2)}, u32[]{:S(2)}) collective-permute-start(f32[8,24,256]{2,1,0:T(8,128)S(1)} %get-tuple-element.46), channel_id=1, source_target_pairs={{0,15},{1,2},{2,1},{3,4},{4,3},{5,6},{6,5},{7,8},{8,7},{9,10},{10,... | collective-permute-start | bytes 589832 | tf_op jit(solution)/shard_map/ppermute | solution.py:622
  12.5 3.5 %copy-start.5 = (s32[1,1,16]{2,1,0:T(1,128)S(1)}, s32[1,1,16]{2,1,0:T(1,128)}, u32[]{:S(2)}) copy-start(s32[1,1,16]{2,1,0:T(1,128)} %active.1) | copy-start | bytes 196
  12.5 5.5 %collective-permute-start.2 = (f32[3,24,256]{2,1,0:T(8,128)S(1)}, f32[3,24,256]{2,1,0:T(8,128)S(1)}, u32[]{:S(2)}, u32[]{:S(2)}) collective-permute-start(f32[3,24,256]{2,1,0:T(8,128)S(1)} %get-tuple-element.40), channel_id=1, source_target_pairs={{0,1},{1,0},{2,3},{3,2},{4,5},{5,4},{6,7},{7,6},{8,9},{9,8},{10,11... | collective-permute-start | bytes 221192 | tf_op jit(solution)/shard_map/ppermute | solution.py:622
  12.6 7.7 %collective-permute-start.3 = (f32[3,24,256]{2,1,0:T(8,128)S(1)}, f32[3,24,256]{2,1,0:T(8,128)S(1)}, u32[]{:S(2)}, u32[]{:S(2)}) collective-permute-start(f32[3,24,256]{2,1,0:T(8,128)S(1)} %get-tuple-element.41), channel_id=1, source_target_pairs={{0,15},{1,2},{2,1},{3,4},{4,3},{5,6},{6,5},{7,8},{8,7},{9,10},{10,... | collective-permute-start | bytes 221192 | tf_op jit(solution)/shard_map/ppermute | solution.py:622
  21.3 8.2 %collective-permute-start.6 = (f32[12,8,128]{2,1,0:T(8,128)S(1)}, f32[12,8,128]{2,1,0:T(8,128)S(1)}, u32[]{:S(2)}, u32[]{:S(2)}) collective-permute-start(f32[12,8,128]{2,1,0:T(8,128)S(1)} %get-tuple-element.56), channel_id=1, source_target_pairs={{0,16},{16,0},{32,48},{48,32},{64,80},{80,64},{96,112},{112,96},{1... | collective-permute-start | bytes 147464 | tf_op jit(solution)/shard_map/ppermute | solution.py:622
  25.8 3.7 %collective-permute-start.7 = (f32[12,8,128]{2,1,0:T(8,128)S(1)}, f32[12,8,128]{2,1,0:T(8,128)S(1)}, u32[]{:S(2)}, u32[]{:S(2)}) collective-permute-start(f32[12,8,128]{2,1,0:T(8,128)S(1)} %get-tuple-element.57), channel_id=1, source_target_pairs={{0,240},{16,32},{32,16},{48,64},{64,48},{80,96},{96,80},{112,128},... | collective-permute-start | bytes 147464 | tf_op jit(solution)/shard_map/ppermute | solution.py:622
  25.8 7.2 %collective-permute-start.8 = (f32[13,8,128]{2,1,0:T(8,128)S(1)}, f32[13,8,128]{2,1,0:T(8,128)S(1)}, u32[]{:S(2)}, u32[]{:S(2)}) collective-permute-start(f32[13,8,128]{2,1,0:T(8,128)S(1)} %get-tuple-element.59), channel_id=1, source_target_pairs={{0,1},{1,0},{2,3},{3,2},{4,5},{5,4},{6,7},{7,6},{8,9},{9,8},{10,11... | collective-permute-start | bytes 159752 | tf_op jit(solution)/shard_map/ppermute | solution.py:622
  25.9 7.1 %collective-permute-start.9 = (f32[13,8,128]{2,1,0:T(8,128)S(1)}, f32[13,8,128]{2,1,0:T(8,128)S(1)}, u32[]{:S(2)}, u32[]{:S(2)}) collective-permute-start(f32[13,8,128]{2,1,0:T(8,128)S(1)} %get-tuple-element.60), channel_id=1, source_target_pairs={{0,15},{1,2},{2,1},{3,4},{4,3},{5,6},{6,5},{7,8},{8,7},{9,10},{10,... | collective-permute-start | bytes 159752 | tf_op jit(solution)/shard_map/ppermute | solution.py:622
  29.5 3.5 %collective-permute-start.10 = (f32[10,8,128]{2,1,0:T(8,128)S(1)}, f32[10,8,128]{2,1,0:T(8,128)S(1)}, u32[]{:S(2)}, u32[]{:S(2)}) collective-permute-start(f32[10,8,128]{2,1,0:T(8,128)S(1)} %get-tuple-element.61), channel_id=1, source_target_pairs={{0,1},{1,0},{2,3},{3,2},{4,5},{5,4},{6,7},{7,6},{8,9},{9,8},{10,11... | collective-permute-start | bytes 122888 | tf_op jit(solution)/shard_map/ppermute | solution.py:622
  29.6 6.3 %collective-permute-start.11 = (f32[10,8,128]{2,1,0:T(8,128)S(1)}, f32[10,8,128]{2,1,0:T(8,128)S(1)}, u32[]{:S(2)}, u32[]{:S(2)}) collective-permute-start(f32[10,8,128]{2,1,0:T(8,128)S(1)} %get-tuple-element.62), channel_id=1, source_target_pairs={{0,15},{1,2},{2,1},{3,4},{4,3},{5,6},{6,5},{7,8},{8,7},{9,10},{10,... | collective-permute-start | bytes 122888 | tf_op jit(solution)/shard_map/ppermute | solution.py:622

commit v3 on v2

--- a/solution.py
+++ b/solution.py
@@ -529,7 +529,7 @@
 def finish(
     gathered, basis, cx_i, cy_i, cz_i, g_i, inv_i, cx_o, cy_o, cz_o, g_o, inv_o,
     resid_i, resid_o, iterate_i, iterate_o, one_x, two_x, one, two, one_out, two_out,
-    out, correction, lift, u0, u1, r0,
+    out, correction,
 ):
     flags = place()
     center, m1, q1, m2, q2 = FINE
@@ -574,8 +574,7 @@
     lanes = (iota((128, LONG), 1) // 4 == iota((128, LONG), 0)).astype(bf16)
     fine = by_right(jnp.concatenate(tall, axis=0), lanes)
     lifted = [fine[RING * a : RING * a + RING] for a in range(6)]
-    for i in range(ROWS):
-        lift[i] = lifted[(i + 1) // 4]
+    lift = [lifted[(i + 1) // 4] for i in range(ROWS)]
 
     none4 = jnp.zeros((4, LONG), f32)
 
@@ -585,7 +584,7 @@
         get, n, k = (own, (x - 2) // 4, (x - 2) % 4) if 2 <= x < 18 else (outer, 0, x if x < 2 else x - 16)
         return jnp.concatenate([get(2 * n + c, pl.ds(2 * k, 2)) for c in range(2)], axis=1)
 
-    for i in range(1, ROWS - 1):
+    def ring_of(i):
         x = i - 1
         if x < 2 or x >= 18:
             get, k = (low, x) if x < 2 else (high, x - 18)
@@ -596,24 +595,22 @@
         else:
             mine = own_layer(x - 2, resid_i, resid_o, 4, 12, 9)
         after, before = strip(right, right_out, x), strip(left, left_out, x)
-        r0[i] = jnp.concatenate([mine, after, none4, before], axis=0)
-
-    for i in range(1, ROWS - 1):
-        r = r0[i] - (g[i] * lift[i] - near(i, lift, cx, cy, cz))
-        r0[i] = r
-        u0[i] = inv[i] * r * (1.0 / center)
-
-    for i in range(2, ROWS - 2):
-        u = u0[i]
-        r = r0[i] - (g[i] * u - near(i, u0, cx, cy, cz))
-        r0[i] = r
-        u1[i] = m1 * u + q1 * (inv[i] * r)
-
-    for i in range(3, 19):
-        u = u1[i]
-        r = r0[i] - (g[i] * u - near(i, u1, cx, cy, cz))
-        step = (u0[i] + u) + (m2 * u + q2 * (inv[i] * r)) + lift[i]
-        out[i - 3] = own_layer(i - 3, iterate_i, iterate_o, 3, 13, 11) + step[:SIDE]
+        return jnp.concatenate([mine, after, none4, before], axis=0)
+
+    r, u0, u1 = {}, {}, {}
+    for k in range(1, ROWS + 1):
+        if k < ROWS - 1:
+            r[k] = ring_of(k) - (g[k] * lift[k] - near(k, lift, cx, cy, cz))
+            u0[k] = inv[k] * r[k] * (1.0 / center)
+        i = k - 1
+        if 2 <= i < ROWS - 2:
+            r[i] = r[i] - (g[i] * u0[i] - near(i, u0, cx, cy, cz))
+            u1[i] = m1 * u0[i] + q1 * (inv[i] * r[i])
+        i = k - 2
+        if 3 <= i < 19:
+            last = r[i] - (g[i] * u1[i] - near(i, u1, cx, cy, cz))
+            step = (u0[i] + u1[i]) + (m2 * u1[i] + q2 * (inv[i] * last)) + lift[i]
+            out[i - 3] = own_layer(i - 3, iterate_i, iterate_o, 3, 13, 11) + step[:SIDE]
 
 
 def swap(values, axis, odd):
@@ -624,7 +621,7 @@
 
 def body(src, cx, cy, cz, ab, active):
     count = lax.axis_size("coarse") * lax.axis_size("fine")
-    block, ring = (SIDE, SIDE, LONG), pltpu.VMEM((ROWS, RING, LONG), f32)
+    block = (SIDE, SIDE, LONG)
 
     first, second = pack_first_call((src, cx, cy, cz, ab))
     one_x, two_x = swap(first, "coarse", False), swap(second, "coarse", True)
@@ -666,11 +663,10 @@
         [pltpu.VMEM((5, 10, 16, 128), f32), pltpu.VMEM((10, 16, 128), f32)],
         ins=[VMEM] * 8,
     )(packed, weight, one_x, two_x, one, two, one_out, two_out)
-    gathered = lax.all_to_all(message[:count], ("coarse", "fine"), 0, 0, tiled=True)
+    gathered = lax.all_to_all(message[:count], ("fine", "coarse"), 0, 0, tiled=True)
     out, correction = call(
         finish,
         [block, (4, 4, 64)],
-        [ring] * 4,
         ins=[VMEM] * 22,
     )(
         gathered, basis, *fields_i, *fields_o, resid_i, resid_o, iterate_i, iterate_o,

time: 63.3 us -> 63.2 us (level)
  no operation moved by 1% of the time
where the time goes in v3:
time: 63.2 us; the launch traced here: 63 us
  blocking collectives  24.3 us (38%)
  starting transfers between devices  23.9 us (38%)
  Pallas kernels  8.18 us (13%)
  waiting for transfers between devices  5.78 us (9%)
  between operations  0.81 us (1%)
    all_to_all x1, blocking collectives, body(): lax.all_to_all(message[:count], ('fine', 'coarse'), 0, 0, tiled=True)  24.3 us
    ppermute x12, starting transfers between devices, swap(): return lax.ppermute(values, axis, list(enumerate(other)))  23.9 us
    ppermute x12, waiting for transfers between devices, swap(): return lax.ppermute(values, axis, list(enumerate(other)))  5.78 us
    pallas_call x1, Pallas kernels, body(): call(finish, [block, (4, 4, 64)], ins=[VMEM] * 22)  2.41 us
    pallas_call x1, Pallas kernels, pack_first_call(): pl.pallas_call(pack_first, out_shape=[jax.ShapeDtypeStruct((16, SIDE, LON...  2.01 us
  transfers between devices with their start and end apart: 12, of which 3 were waited for; matrix products, arithmetic and copies ran while one was open for 0% of the time, Pallas kernels for 4%

profile of v3, /device:TPU:1, one launch (start us, length us, event | category | flops | bytes accessed | tf_op | source)
XLA Modules:
  0.0 63.0 jit_solution(6518234292043130377)
XLA Ops:
  0.6 0.0 copy-start.2
  0.6 0.0 copy-start.1
  0.7 0.0 copy-start
  0.7 0.0 copy-start.3
  0.7 0.0 copy-start.4
  0.7 2.0 %shard_map.77 = (f32[16,16,256]{2,1,0:T(8,128)}, f32[16,16,256]{2,1,0:T(8,128)}) custom-call(f32[16,16,256]{2,1,0:T(8,128)} %src.7, f32[16,16,256]{2,1,0:T(8,128)} %cx.9, f32[16,16,256]{2,1,0:T(8,128)} %cy.9, f32[16,16,256]{2,1,0:T(8,128)} %cz.9, f32[16,16,256]{2,1,0:T(8,128)} %ab.5), custom_call_target="tpu_custom_call" | custom-call | tf_op jit(solution)/shard_map/pallas_call | solution.py:90
  2.7 3.3 %collective-permute-start = (f32[16,16,256]{2,1,0:T(8,128)}, f32[16,16,256]{2,1,0:T(8,128)S(1)}, u32[]{:S(2)}, u32[]{:S(2)}) collective-permute-start(f32[16,16,256]{2,1,0:T(8,128)} %get-tuple-element.37), channel_id=1, source_target_pairs={{0,16},{16,0},{32,48},{48,32},{64,80},{80,64},{96,112},{112,96},{1... | collective-permute-start | bytes 786440 | tf_op jit(solution)/shard_map/ppermute | solution.py:619
  6.0 0.0 collective-permute-start.1
  6.0 0.0 copy-done.2
  6.0 0.0 copy-done.1
  6.0 0.0 copy-done
  6.0 0.0 copy-done.3
  6.0 0.0 copy-done.4
  6.1 0.2 shard_map.80
  6.3 1.2 %collective-permute-start.4 = (f32[8,24,256]{2,1,0:T(8,128)S(1)}, f32[8,24,256]{2,1,0:T(8,128)S(1)}, u32[]{:S(2)}, u32[]{:S(2)}) collective-permute-start(f32[8,24,256]{2,1,0:T(8,128)S(1)} %get-tuple-element.45), channel_id=1, source_target_pairs={{0,1},{1,0},{2,3},{3,2},{4,5},{5,4},{6,7},{7,6},{8,9},{9,8},{10,11... | collective-permute-start | bytes 589832 | tf_op jit(solution)/shard_map/ppermute | solution.py:619
  7.5 4.3 %collective-permute-start.5 = (f32[8,24,256]{2,1,0:T(8,128)S(1)}, f32[8,24,256]{2,1,0:T(8,128)S(1)}, u32[]{:S(2)}, u32[]{:S(2)}) collective-permute-start(f32[8,24,256]{2,1,0:T(8,128)S(1)} %get-tuple-element.46), channel_id=1, source_target_pairs={{0,15},{1,2},{2,1},{3,4},{4,3},{5,6},{6,5},{7,8},{8,7},{9,10},{10,... | collective-permute-start | bytes 589832 | tf_op jit(solution)/shard_map/ppermute | solution.py:619
  11.7 0.0 collective-permute-done.one.one_x
  11.7 0.6 collective-permute-done.1.two.two_x
  12.3 0.1 shard_map.78
  12.5 0.0 copy-start.5
  12.5 0.1 collective-permute-start.2
  12.6 3.4 %collective-permute-start.3 = (f32[3,24,256]{2,1,0:T(8,128)S(1)}, f32[3,24,256]{2,1,0:T(8,128)S(1)}, u32[]{:S(2)}, u32[]{:S(2)}) collective-permute-start(f32[3,24,256]{2,1,0:T(8,128)S(1)} %get-tuple-element.41), channel_id=1, source_target_pairs={{0,15},{1,2},{2,1},{3,4},{4,3},{5,6},{6,5},{7,8},{8,7},{9,10},{10,... | collective-permute-start | bytes 221192 | tf_op jit(solution)/shard_map/ppermute | solution.py:619
  16.0 0.0 copy-done.5
  16.0 0.9 %shard_map.79 = (f32[4,4,8,128]{3,2,1,0:T(8,128)S(1)}, f32[8,128]{1,0:T(8,128)S(1)}) custom-call(f32[16,16,256]{2,1,0:T(8,128)S(1)} %copy-done, f32[16,16,256]{2,1,0:T(8,128)S(1)} %copy-done.1, f32[16,16,256]{2,1,0:T(8,128)S(1)} %copy-done.2, f32[16,16,256]{2,1,0:T(8,128)S(1)} %copy-done.4, s32[1,1,16]{2,1,0:T(1,128)S(1)} %copy-done.5), custom_call_target="tpu_custom_call" | custom-call | tf_op jit(solution)/shard_map/pallas_call | solution.py:628
  16.9 0.0 collective-permute-done.4.one
  16.9 0.0 collective-permute-done.5.two
  17.0 1.0 %shard_map.81 = (f32[15,24,256]{2,1,0:T(8,128)S(1)}, f32[15,24,256]{2,1,0:T(8,128)S(1)}, f32[15,24,256]{2,1,0:T(8,128)S(1)}, f32[15,24,256]{2,1,0:T(8,128)S(1)},...) custom-call(f32[16,16,256]{2,1,0:T(8,128)S(1)} %copy-done.3, ...), custom_call_target="tpu_custom_call" | custom-call | tf_op jit(solution)/shard_map/pallas_call | solution.py:638
  18.0 0.0 collective-permute-done.2.one
  18.0 2.3 %collective-permute-done.3.two = f32[3,24,256]{2,1,0:T(8,128)S(1)} collective-permute-done((f32[3,24,256]{2,1,0:T(8,128)S(1)}, f32[3,24,256]{2,1,0:T(8,128)S(1)}, u32[]{:S(2)}, u32[]{:S(2)}) %collective-permute-start.3) | collective-permute-done | bytes 73760 | tf_op jit(solution)/shard_map/ppermute | solution.py:619
  20.3 1.0 %shard_map.82 = (f32[7,24,256]{2,1,0:T(8,128)S(1)}, f32[7,24,256]{2,1,0:T(8,128)S(1)}, f32[7,24,256]{2,1,0:T(8,128)S(1)}, f32[7,24,256]{2,1,0:T(8,128)S(1)}, f32...) custom-call(f32[16,16,256]{2,1,0:T(8,128)S(1)} %copy-done.3, ...), custom_call_target="tpu_custom_call" | custom-call | tf_op jit(solution)/shard_map/pallas_call | solution.py:644
  21.3 4.5 %collective-permute-start.6 = (f32[12,8,128]{2,1,0:T(8,128)S(1)}, f32[12,8,128]{2,1,0:T(8,128)S(1)}, u32[]{:S(2)}, u32[]{:S(2)}) collective-permute-start(f32[12,8,128]{2,1,0:T(8,128)S(1)} %get-tuple-element.56), channel_id=1, source_target_pairs={{0,16},{16,0},{32,48},{48,32},{64,80},{80,64},{96,112},{112,96},{1... | collective-permute-start | bytes 147464 | tf_op jit(solution)/shard_map/ppermute | solution.py:619
  25.8 0.0 collective-permute-start.7
  25.8 0.1 collective-permute-start.8
  25.9 3.6 %collective-permute-start.9 = (f32[13,8,128]{2,1,0:T(8,128)S(1)}, f32[13,8,128]{2,1,0:T(8,128)S(1)}, u32[]{:S(2)}, u32[]{:S(2)}) collective-permute-start(f32[13,8,128]{2,1,0:T(8,128)S(1)} %get-tuple-element.60), channel_id=1, source_target_pairs={{0,15},{1,2},{2,1},{3,4},{4,3},{5,6},{6,5},{7,8},{8,7},{9,10},{10,... | collective-permute-start | bytes 159752 | tf_op jit(solution)/shard_map/ppermute | solution.py:619
  29.5 0.0 collective-permute-done.6.one_x
  29.5 0.0 collective-permute-done.7.two_x
  29.5 0.1 collective-permute-start.10
  29.6 3.4 %collective-permute-start.11 = (f32[10,8,128]{2,1,0:T(8,128)S(1)}, f32[10,8,128]{2,1,0:T(8,128)S(1)}, u32[]{:S(2)}, u32[]{:S(2)}) collective-permute-start(f32[10,8,128]{2,1,0:T(8,128)S(1)} %get-tuple-element.62), channel_id=1, source_target_pairs={{0,15},{1,2},{2,1},{3,4},{4,3},{5,6},{6,5},{7,8},{8,7},{9,10},{10,... | collective-permute-start | bytes 122888 | tf_op jit(solution)/shard_map/ppermute | solution.py:619
  33.0 0.0 collective-permute-done.8.one
  33.0 0.0 collective-permute-done.9.two
  33.0 0.0 collective-permute-done.10.one_out
  33.0 2.9 %collective-permute-done.11.two_out = f32[10,8,128]{2,1,0:T(8,128)S(1)} collective-permute-done((f32[10,8,128]{2,1,0:T(8,128)S(1)}, f32[10,8,128]{2,1,0:T(8,128)S(1)}, u32[]{:S(2)}, u32[]{:S(2)}) %collective-permute-start.11) | collective-permute-done | bytes 40992 | tf_op jit(solution)/shard_map/ppermute | solution.py:619
  35.9 0.4 shard_map.85
  36.3 24.3 %all_to_all.11 = f32[256,1,128]{2,1,0:T(1,128)S(1)} all-to-all(f32[256,1,128]{2,1,0:T(1,128)S(1)} %bitcast.5), channel_id=1, replica_groups=mesh['coarse'=16,'fine'=16] {'fine','coarse'}, dimensions={0} | all-to-all | bytes 262144 | tf_op jit(solution)/shard_map/all_to_all | solution.py:666
  60.6 2.4 %shard_map.86 = (f32[16,16,256]{2,1,0:T(8,128)}, f32[4,4,64]{2,1,0:T(4,128)}) custom-call(f32[256,128]{1,0:T(8,128)S(1)} %bitcast.4, f32[3,6,16,128]{3,2,1,0:T(8,128)S(1)} %get-tuple-element.64.basis, f32[15,24,256]{2,1,0:T(8,128)S(1)} %get-tuple-element.47.cx_i, f32[15,24,256]{2,1,0:T(8,128)S(1)} %get-tuple-element.48.cy_i, ...), custom_call_target="tpu_custom_call" | custom-call | tf_op jit(solution)/shard_map/pallas_call | solution.py:667
  (2 shorter events, 0.1 us)
Async XLA Ops:
  0.6 5.4 %copy-start.2 = (f32[16,16,256]{2,1,0:T(8,128)S(1)}, f32[16,16,256]{2,1,0:T(8,128)}, u32[]{:S(2)}) copy-start(f32[16,16,256]{2,1,0:T(8,128)} %cz.9) | copy-start | bytes 786436
  0.6 5.4 %copy-start.1 = (f32[16,16,256]{2,1,0:T(8,128)S(1)}, f32[16,16,256]{2,1,0:T(8,128)}, u32[]{:S(2)}) copy-start(f32[16,16,256]{2,1,0:T(8,128)} %cy.9) | copy-start | bytes 786436
  0.7 5.4 %copy-start = (f32[16,16,256]{2,1,0:T(8,128)S(1)}, f32[16,16,256]{2,1,0:T(8,128)}, u32[]{:S(2)}) copy-start(f32[16,16,256]{2,1,0:T(8,128)} %cx.9) | copy-start | bytes 786436
  0.7 5.4 %copy-start.3 = (f32[16,16,256]{2,1,0:T(8,128)S(1)}, f32[16,16,256]{2,1,0:T(8,128)}, u32[]{:S(2)}) copy-start(f32[16,16,256]{2,1,0:T(8,128)} %src.7) | copy-start | bytes 786436
  0.7 5.4 %copy-start.4 = (f32[16,16,256]{2,1,0:T(8,128)S(1)}, f32[16,16,256]{2,1,0:T(8,128)}, u32[]{:S(2)}) copy-start(f32[16,16,256]{2,1,0:T(8,128)} %ab.5) | copy-start | bytes 786436
  2.7 9.0 %collective-permute-start = (f32[16,16,256]{2,1,0:T(8,128)}, f32[16,16,256]{2,1,0:T(8,128)S(1)}, u32[]{:S(2)}, u32[]{:S(2)}) collective-permute-start(f32[16,16,256]{2,1,0:T(8,128)} %get-tuple-element.37), channel_id=1, source_target_pairs={{0,16},{16,0},{32,48},{48,32},{64,80},{80,64},{96,112},{112,96},{1... | collective-permute-start | bytes 786440 | tf_op jit(solution)/shard_map/ppermute | solution.py:619
  6.0 6.3 %collective-permute-start.1 = (f32[16,16,256]{2,1,0:T(8,128)}, f32[16,16,256]{2,1,0:T(8,128)S(1)}, u32[]{:S(2)}, u32[]{:S(2)}) collective-permute-start(f32[16,16,256]{2,1,0:T(8,128)} %get-tuple-element.38), channel_id=1, source_target_pairs={{0,240},{16,32},{32,16},{48,64},{64,48},{80,96},{96,80},{112,128},... | collective-permute-start | bytes 786440 | tf_op jit(solution)/shard_map/ppermute | solution.py:619
  6.3 10.6 %collective-permute-start.4 = (f32[8,24,256]{2,1,0:T(8,128)S(1)}, f32[8,24,256]{2,1,0:T(8,128)S(1)}, u32[]{:S(2)}, u32[]{:S(2)}) collective-permute-start(f32[8,24,256]{2,1,0:T(8,128)S(1)} %get-tuple-element.45), channel_id=1, source_target_pairs={{0,1},{1,0},{2,3},{3,2},{4,5},{5,4},{6,7},{7,6},{8,9},{9,8},{10,11... | collective-permute-start | bytes 589832 | tf_op jit(solution)/shard_map/ppermute | solution.py:619
  7.5 9.5 %collective-permute-start.5 = (f32[8,24,256]{2,1,0:T(8,128)S(1)}, f32[8,24,256]{2,1,0:T(8,128)S(1)}, u32[]{:S(2)}, u32[]{:S(2)}) collective-permute-start(f32[8,24,256]{2,1,0:T(8,128)S(1)} %get-tuple-element.46), channel_id=1, source_target_pairs={{0,15},{1,2},{2,1},{3,4},{4,3},{5,6},{6,5},{7,8},{8,7},{9,10},{10,... | collective-permute-start | bytes 589832 | tf_op jit(solution)/shard_map/ppermute | solution.py:619
  12.5 3.5 %copy-start.5 = (s32[1,1,16]{2,1,0:T(1,128)S(1)}, s32[1,1,16]{2,1,0:T(1,128)}, u32[]{:S(2)}) copy-start(s32[1,1,16]{2,1,0:T(1,128)} %active.1) | copy-start | bytes 196
  12.5 5.5 %collective-permute-start.2 = (f32[3,24,256]{2,1,0:T(8,128)S(1)}, f32[3,24,256]{2,1,0:T(8,128)S(1)}, u32[]{:S(2)}, u32[]{:S(2)}) collective-permute-start(f32[3,24,256]{2,1,0:T(8,128)S(1)} %get-tuple-element.40), channel_id=1, source_target_pairs={{0,1},{1,0},{2,3},{3,2},{4,5},{5,4},{6,7},{7,6},{8,9},{9,8},{10,11... | collective-permute-start | bytes 221192 | tf_op jit(solution)/shard_map/ppermute | solution.py:619
  12.6 7.7 %collective-permute-start.3 = (f32[3,24,256]{2,1,0:T(8,128)S(1)}, f32[3,24,256]{2,1,0:T(8,128)S(1)}, u32[]{:S(2)}, u32[]{:S(2)}) collective-permute-start(f32[3,24,256]{2,1,0:T(8,128)S(1)} %get-tuple-element.41), channel_id=1, source_target_pairs={{0,15},{1,2},{2,1},{3,4},{4,3},{5,6},{6,5},{7,8},{8,7},{9,10},{10,... | collective-permute-start | bytes 221192 | tf_op jit(solution)/shard_map/ppermute | solution.py:619
  21.3 8.2 %collective-permute-start.6 = (f32[12,8,128]{2,1,0:T(8,128)S(1)}, f32[12,8,128]{2,1,0:T(8,128)S(1)}, u32[]{:S(2)}, u32[]{:S(2)}) collective-permute-start(f32[12,8,128]{2,1,0:T(8,128)S(1)} %get-tuple-element.56), channel_id=1, source_target_pairs={{0,16},{16,0},{32,48},{48,32},{64,80},{80,64},{96,112},{112,96},{1... | collective-permute-start | bytes 147464 | tf_op jit(solution)/shard_map/ppermute | solution.py:619
  25.8 3.7 %collective-permute-start.7 = (f32[12,8,128]{2,1,0:T(8,128)S(1)}, f32[12,8,128]{2,1,0:T(8,128)S(1)}, u32[]{:S(2)}, u32[]{:S(2)}) collective-permute-start(f32[12,8,128]{2,1,0:T(8,128)S(1)} %get-tuple-element.57), channel_id=1, source_target_pairs={{0,240},{16,32},{32,16},{48,64},{64,48},{80,96},{96,80},{112,128},... | collective-permute-start | bytes 147464 | tf_op jit(solution)/shard_map/ppermute | solution.py:619
  25.8 7.2 %collective-permute-start.8 = (f32[13,8,128]{2,1,0:T(8,128)S(1)}, f32[13,8,128]{2,1,0:T(8,128)S(1)}, u32[]{:S(2)}, u32[]{:S(2)}) collective-permute-start(f32[13,8,128]{2,1,0:T(8,128)S(1)} %get-tuple-element.59), channel_id=1, source_target_pairs={{0,1},{1,0},{2,3},{3,2},{4,5},{5,4},{6,7},{7,6},{8,9},{9,8},{10,11... | collective-permute-start | bytes 159752 | tf_op jit(solution)/shard_map/ppermute | solution.py:619
  25.9 7.1 %collective-permute-start.9 = (f32[13,8,128]{2,1,0:T(8,128)S(1)}, f32[13,8,128]{2,1,0:T(8,128)S(1)}, u32[]{:S(2)}, u32[]{:S(2)}) collective-permute-start(f32[13,8,128]{2,1,0:T(8,128)S(1)} %get-tuple-element.60), channel_id=1, source_target_pairs={{0,15},{1,2},{2,1},{3,4},{4,3},{5,6},{6,5},{7,8},{8,7},{9,10},{10,... | collective-permute-start | bytes 159752 | tf_op jit(solution)/shard_map/ppermute | solution.py:619
  29.5 3.5 %collective-permute-start.10 = (f32[10,8,128]{2,1,0:T(8,128)S(1)}, f32[10,8,128]{2,1,0:T(8,128)S(1)}, u32[]{:S(2)}, u32[]{:S(2)}) collective-permute-start(f32[10,8,128]{2,1,0:T(8,128)S(1)} %get-tuple-element.61), channel_id=1, source_target_pairs={{0,1},{1,0},{2,3},{3,2},{4,5},{5,4},{6,7},{7,6},{8,9},{9,8},{10,11... | collective-permute-start | bytes 122888 | tf_op jit(solution)/shard_map/ppermute | solution.py:619
  29.6 6.3 %collective-permute-start.11 = (f32[10,8,128]{2,1,0:T(8,128)S(1)}, f32[10,8,128]{2,1,0:T(8,128)S(1)}, u32[]{:S(2)}, u32[]{:S(2)}) collective-permute-start(f32[10,8,128]{2,1,0:T(8,128)S(1)} %get-tuple-element.62), channel_id=1, source_target_pairs={{0,15},{1,2},{2,1},{3,4},{4,3},{5,6},{6,5},{7,8},{8,7},{9,10},{10,... | collective-permute-start | bytes 122888 | tf_op jit(solution)/shard_map/ppermute | solution.py:619

commit v4 on v3

--- a/solution.py
+++ b/solution.py
@@ -287,7 +287,7 @@
 
 def smooth_inner(
     src, cx, cy, cz, diag, one, two,
-    cx_o, cy_o, cz_o, g_o, inv_o, edge, iterate, resid, u0, u1, u2, r,
+    cx_o, cy_o, cz_o, g_o, inv_o, edge, iterate, resid, rhs, u0, u1, u2, r,
 ):
     flags = place()
     center, m1, q1, m2, q2 = FINE
@@ -316,13 +316,18 @@
     for values, rows in zip((r, u0, u1, u2), EDGES):
         for i, at in rows.items():
             edge[at] = values[i]
-    for i in range(7, 16):
-        resid[i - 7] = (r[i] - (g[i] * u2[i] - near(i, u2, cx, cy, cz)))[:SIDE]
+    made = [(r[i] - (g[i] * u2[i] - near(i, u2, cx, cy, cz)))[:SIDE] for i in range(7, 16)]
+    for k, value in enumerate(made):
+        resid[k] = value
+    totals = [(made[k] + made[k + 1]) + (made[k + 2] + made[k + 3]) for k in (0, 4)]
+    total = by_right(jnp.concatenate(totals, axis=0), sum_lanes(False))
+    for k in range(2):
+        rhs[k] = by_left(sum_rows(False), total[SIDE * k : SIDE * k + SIDE])
 
 
 def smooth_outer(
     src, cx, cy, cz, one_x, two_x, diag, one, two, coarse, active,
-    cx_i, cy_i, cz_i, g_i, inv_i, edge, resid_i,
+    cx_i, cy_i, cz_i, g_i, inv_i, edge, resid_i, rhs_i,
     cx_o, cy_o, cz_o, g_o, inv_o, iterate, resid, packed, weight, first, second,
 ):
     flags = place()
@@ -391,7 +396,7 @@
         resid[k] = edges[i - 3]
     even = flags[5] > 0
     rest = [edges[x] if x in edges else resid_i[x - 4] for x in range(SIDE)]
-    totals = [(rest[x] + rest[x + 1]) + (rest[x + 2] + rest[x + 3]) for x in range(0, SIDE, 4)]
+    totals = [(rest[x] + rest[x + 1]) + (rest[x + 2] + rest[x + 3]) for x in (0, 12)]
 
     for k in range(2):
         up, down = edges[14 + k], edges[k]
@@ -402,7 +407,12 @@
             second[4 * k + n] = jnp.where(even, q, p)
     rhs = by_right(jnp.concatenate(totals, axis=0), lanes)
     for a in range(4):
-        tiles[a] = tiles[a] + inverse[a] * by_left(rows, rhs[SIDE * a : SIDE * a + SIDE])
+        if a in (1, 2):
+            here = rhs_i[a - 1]
+        else:
+            at = 0 if a == 0 else SIDE
+            here = by_left(rows, rhs[at : at + SIDE])
+        tiles[a] = tiles[a] + inverse[a] * here
         packed[a] = tiles[a]
     ups, downs = tiles[1:4] + [join(uppers[1:4])], tiles[0:3] + [join(uppers[0:3])]
     for k, (p, q) in enumerate(zip(ups, downs)):
@@ -635,9 +645,9 @@
     )(src, cx, cy, cz, ab, one_x, two_x)
     one_out, two_out = swap(first, "fine", False), swap(second, "fine", True)
     inner, outer = (15, RING, LONG), (7, RING, LONG)
-    *fields_i, edge, iterate_i, resid_i = call(
+    *fields_i, edge, iterate_i, resid_i, rhs_i = call(
         smooth_inner,
-        [inner] * 5 + [(18, RING, LONG), (11, SIDE, LONG), (9, SIDE, LONG)],
+        [inner] * 5 + [(18, RING, LONG), (11, SIDE, LONG), (9, SIDE, LONG), (2, 8, 128)],
         [pltpu.VMEM(inner, f32)] * 4,
         ins=[VMEM] * 7,
     )(src, cx, cy, cz, diag, one, two)
@@ -645,10 +655,10 @@
         smooth_outer,
         [outer] * 5 + [(5, SIDE, LONG), (7, SIDE, LONG)]
         + [(5, 8, 128), (4, 8, 128), (12, 8, 128), (12, 8, 128)],
-        ins=[VMEM] * 18,
+        ins=[VMEM] * 19,
     )(
         src, cx, cy, cz, one_x, two_x, diag_out, one_out, two_out, coarse, mask,
-        *fields_i, edge, resid_i,
+        *fields_i, edge, resid_i, rhs_i,
     )
     one_x, two_x = swap(first, "coarse", False), swap(second, "coarse", True)
     first, second = call(pack_own, [(13, 8, 128)] * 2, ins=[VMEM] * 3)(

time: 63.2 us -> 63.1 us (level)
  no operation moved by 1% of the time
where the time goes in v4:
time: 63.1 us; the launch traced here: 62.9 us
  blocking collectives  24.3 us (39%)
  starting transfers between devices  23.9 us (38%)
  Pallas kernels  8.34 us (13%)
  waiting for transfers between devices  5.56 us (9%)
  between operations  0.8 us (1%)
    all_to_all x1, blocking collectives, body(): lax.all_to_all(message[:count], ('fine', 'coarse'), 0, 0, tiled=True)  24.3 us
    ppermute x12, starting transfers between devices, swap(): return lax.ppermute(values, axis, list(enumerate(other)))  23.9 us
    ppermute x12, waiting for transfers between devices, swap(): return lax.ppermute(values, axis, list(enumerate(other)))  5.56 us
    pallas_call x1, Pallas kernels, body(): call(finish, [block, (4, 4, 64)], ins=[VMEM] * 22)  2.39 us
    pallas_call x1, Pallas kernels, pack_first_call(): pl.pallas_call(pack_first, out_shape=[jax.ShapeDtypeStruct((16, SIDE, LON...  2.01 us
  transfers between devices with their start and end apart: 12, of which 3 were waited for; matrix products, arithmetic and copies ran while one was open for 0% of the time, Pallas kernels for 4%

profile of v4, /device:TPU:1, one launch (start us, length us, event | category | flops | bytes accessed | tf_op | source)
XLA Modules:
  0.0 62.9 jit_solution(1055789661641663381)
XLA Ops:
  0.6 0.0 copy-start.2
  0.6 0.0 copy-start.1
  0.7 0.0 copy-start
  0.7 0.0 copy-start.3
  0.7 0.0 copy-start.4
  0.7 2.0 %shard_map.77 = (f32[16,16,256]{2,1,0:T(8,128)}, f32[16,16,256]{2,1,0:T(8,128)}) custom-call(f32[16,16,256]{2,1,0:T(8,128)} %src.7, f32[16,16,256]{2,1,0:T(8,128)} %cx.9, f32[16,16,256]{2,1,0:T(8,128)} %cy.9, f32[16,16,256]{2,1,0:T(8,128)} %cz.9, f32[16,16,256]{2,1,0:T(8,128)} %ab.5), custom_call_target="tpu_custom_call" | custom-call | tf_op jit(solution)/shard_map/pallas_call | solution.py:90
  2.7 3.3 %collective-permute-start = (f32[16,16,256]{2,1,0:T(8,128)}, f32[16,16,256]{2,1,0:T(8,128)S(1)}, u32[]{:S(2)}, u32[]{:S(2)}) collective-permute-start(f32[16,16,256]{2,1,0:T(8,128)} %get-tuple-element.38), channel_id=1, source_target_pairs={{0,16},{16,0},{32,48},{48,32},{64,80},{80,64},{96,112},{112,96},{1... | collective-permute-start | bytes 786440 | tf_op jit(solution)/shard_map/ppermute | solution.py:629
  6.0 0.0 collective-permute-start.1
  6.0 0.0 copy-done.2
  6.0 0.0 copy-done.1
  6.0 0.0 copy-done
  6.0 0.0 copy-done.3
  6.0 0.0 copy-done.4
  6.1 0.2 shard_map.80
  6.3 1.2 %collective-permute-start.4 = (f32[8,24,256]{2,1,0:T(8,128)S(1)}, f32[8,24,256]{2,1,0:T(8,128)S(1)}, u32[]{:S(2)}, u32[]{:S(2)}) collective-permute-start(f32[8,24,256]{2,1,0:T(8,128)S(1)} %get-tuple-element.46), channel_id=1, source_target_pairs={{0,1},{1,0},{2,3},{3,2},{4,5},{5,4},{6,7},{7,6},{8,9},{9,8},{10,11... | collective-permute-start | bytes 589832 | tf_op jit(solution)/shard_map/ppermute | solution.py:629
  7.5 4.3 %collective-permute-start.5 = (f32[8,24,256]{2,1,0:T(8,128)S(1)}, f32[8,24,256]{2,1,0:T(8,128)S(1)}, u32[]{:S(2)}, u32[]{:S(2)}) collective-permute-start(f32[8,24,256]{2,1,0:T(8,128)S(1)} %get-tuple-element.47), channel_id=1, source_target_pairs={{0,15},{1,2},{2,1},{3,4},{4,3},{5,6},{6,5},{7,8},{8,7},{9,10},{10,... | collective-permute-start | bytes 589832 | tf_op jit(solution)/shard_map/ppermute | solution.py:629
  11.7 0.0 collective-permute-done.one.one_x
  11.7 0.6 collective-permute-done.1.two.two_x
  12.3 0.1 shard_map.78
  12.5 0.0 copy-start.5
  12.5 0.1 collective-permute-start.2
  12.6 3.4 %collective-permute-start.3 = (f32[3,24,256]{2,1,0:T(8,128)S(1)}, f32[3,24,256]{2,1,0:T(8,128)S(1)}, u32[]{:S(2)}, u32[]{:S(2)}) collective-permute-start(f32[3,24,256]{2,1,0:T(8,128)S(1)} %get-tuple-element.42), channel_id=1, source_target_pairs={{0,15},{1,2},{2,1},{3,4},{4,3},{5,6},{6,5},{7,8},{8,7},{9,10},{10,... | collective-permute-start | bytes 221192 | tf_op jit(solution)/shard_map/ppermute | solution.py:629
  16.0 0.0 copy-done.5
  16.0 0.9 %shard_map.79 = (f32[4,4,8,128]{3,2,1,0:T(8,128)S(1)}, f32[8,128]{1,0:T(8,128)S(1)}) custom-call(f32[16,16,256]{2,1,0:T(8,128)S(1)} %copy-done, f32[16,16,256]{2,1,0:T(8,128)S(1)} %copy-done.1, f32[16,16,256]{2,1,0:T(8,128)S(1)} %copy-done.2, f32[16,16,256]{2,1,0:T(8,128)S(1)} %copy-done.4, s32[1,1,16]{2,1,0:T(1,128)S(1)} %copy-done.5), custom_call_target="tpu_custom_call" | custom-call | tf_op jit(solution)/shard_map/pallas_call | solution.py:638
  16.9 0.0 collective-permute-done.4.one
  16.9 0.0 collective-permute-done.5.two
  17.0 1.3 %shard_map.81 = (f32[15,24,256]{2,1,0:T(8,128)S(1)}, f32[15,24,256]{2,1,0:T(8,128)S(1)}, f32[15,24,256]{2,1,0:T(8,128)S(1)}, f32[15,24,256]{2,1,0:T(8,128)S(1)},...) custom-call(f32[16,16,256]{2,1,0:T(8,128)S(1)} %copy-done.3, ...), custom_call_target="tpu_custom_call" | custom-call | tf_op jit(solution)/shard_map/pallas_call | solution.py:648
  18.2 0.0 collective-permute-done.2.one
  18.2 2.1 %collective-permute-done.3.two = f32[3,24,256]{2,1,0:T(8,128)S(1)} collective-permute-done((f32[3,24,256]{2,1,0:T(8,128)S(1)}, f32[3,24,256]{2,1,0:T(8,128)S(1)}, u32[]{:S(2)}, u32[]{:S(2)}) %collective-permute-start.3) | collective-permute-done | bytes 73760 | tf_op jit(solution)/shard_map/ppermute | solution.py:629
  20.3 0.9 %shard_map.82 = (f32[7,24,256]{2,1,0:T(8,128)S(1)}, f32[7,24,256]{2,1,0:T(8,128)S(1)}, f32[7,24,256]{2,1,0:T(8,128)S(1)}, f32[7,24,256]{2,1,0:T(8,128)S(1)}, f32...) custom-call(f32[16,16,256]{2,1,0:T(8,128)S(1)} %copy-done.3, ...), custom_call_target="tpu_custom_call" | custom-call | tf_op jit(solution)/shard_map/pallas_call | solution.py:654
  21.2 4.5 %collective-permute-start.6 = (f32[12,8,128]{2,1,0:T(8,128)S(1)}, f32[12,8,128]{2,1,0:T(8,128)S(1)}, u32[]{:S(2)}, u32[]{:S(2)}) collective-permute-start(f32[12,8,128]{2,1,0:T(8,128)S(1)} %get-tuple-element.58), channel_id=1, source_target_pairs={{0,16},{16,0},{32,48},{48,32},{64,80},{80,64},{96,112},{112,96},{1... | collective-permute-start | bytes 147464 | tf_op jit(solution)/shard_map/ppermute | solution.py:629
  25.7 0.0 collective-permute-start.7
  25.7 0.1 collective-permute-start.8
  25.8 3.6 %collective-permute-start.9 = (f32[13,8,128]{2,1,0:T(8,128)S(1)}, f32[13,8,128]{2,1,0:T(8,128)S(1)}, u32[]{:S(2)}, u32[]{:S(2)}) collective-permute-start(f32[13,8,128]{2,1,0:T(8,128)S(1)} %get-tuple-element.62), channel_id=1, source_target_pairs={{0,15},{1,2},{2,1},{3,4},{4,3},{5,6},{6,5},{7,8},{8,7},{9,10},{10,... | collective-permute-start | bytes 159752 | tf_op jit(solution)/shard_map/ppermute | solution.py:629
  29.4 0.0 collective-permute-done.6.one_x
  29.4 0.0 collective-permute-done.7.two_x
  29.5 0.1 collective-permute-start.10
  29.6 3.4 %collective-permute-start.11 = (f32[10,8,128]{2,1,0:T(8,128)S(1)}, f32[10,8,128]{2,1,0:T(8,128)S(1)}, u32[]{:S(2)}, u32[]{:S(2)}) collective-permute-start(f32[10,8,128]{2,1,0:T(8,128)S(1)} %get-tuple-element.64), channel_id=1, source_target_pairs={{0,15},{1,2},{2,1},{3,4},{4,3},{5,6},{6,5},{7,8},{8,7},{9,10},{10,... | collective-permute-start | bytes 122888 | tf_op jit(solution)/shard_map/ppermute | solution.py:629
  32.9 0.0 collective-permute-done.8.one
  32.9 0.0 collective-permute-done.9.two
  32.9 0.0 collective-permute-done.10.one_out
  32.9 2.9 %collective-permute-done.11.two_out = f32[10,8,128]{2,1,0:T(8,128)S(1)} collective-permute-done((f32[10,8,128]{2,1,0:T(8,128)S(1)}, f32[10,8,128]{2,1,0:T(8,128)S(1)}, u32[]{:S(2)}, u32[]{:S(2)}) %collective-permute-start.11) | collective-permute-done | bytes 40992 | tf_op jit(solution)/shard_map/ppermute | solution.py:629
  35.8 0.4 shard_map.85
  36.3 24.3 %all_to_all.11 = f32[256,1,128]{2,1,0:T(1,128)S(1)} all-to-all(f32[256,1,128]{2,1,0:T(1,128)S(1)} %bitcast.5), channel_id=1, replica_groups=mesh['coarse'=16,'fine'=16] {'fine','coarse'}, dimensions={0} | all-to-all | bytes 262144 | tf_op jit(solution)/shard_map/all_to_all | solution.py:676
  60.6 2.4 %shard_map.86 = (f32[16,16,256]{2,1,0:T(8,128)}, f32[4,4,64]{2,1,0:T(4,128)}) custom-call(f32[256,128]{1,0:T(8,128)S(1)} %bitcast.4, f32[3,6,16,128]{3,2,1,0:T(8,128)S(1)} %get-tuple-element.66.basis, f32[15,24,256]{2,1,0:T(8,128)S(1)} %get-tuple-element.48.cx_i, f32[15,24,256]{2,1,0:T(8,128)S(1)} %get-tuple-element.49.cy_i, ...), custom_call_target="tpu_custom_call" | custom-call | tf_op jit(solution)/shard_map/pallas_call | solution.py:677
  (2 shorter events, 0.1 us)
Async XLA Ops:
  0.6 5.4 %copy-start.2 = (f32[16,16,256]{2,1,0:T(8,128)S(1)}, f32[16,16,256]{2,1,0:T(8,128)}, u32[]{:S(2)}) copy-start(f32[16,16,256]{2,1,0:T(8,128)} %cz.9) | copy-start | bytes 786436
  0.6 5.4 %copy-start.1 = (f32[16,16,256]{2,1,0:T(8,128)S(1)}, f32[16,16,256]{2,1,0:T(8,128)}, u32[]{:S(2)}) copy-start(f32[16,16,256]{2,1,0:T(8,128)} %cy.9) | copy-start | bytes 786436
  0.7 5.4 %copy-start = (f32[16,16,256]{2,1,0:T(8,128)S(1)}, f32[16,16,256]{2,1,0:T(8,128)}, u32[]{:S(2)}) copy-start(f32[16,16,256]{2,1,0:T(8,128)} %cx.9) | copy-start | bytes 786436
  0.7 5.4 %copy-start.3 = (f32[16,16,256]{2,1,0:T(8,128)S(1)}, f32[16,16,256]{2,1,0:T(8,128)}, u32[]{:S(2)}) copy-start(f32[16,16,256]{2,1,0:T(8,128)} %src.7) | copy-start | bytes 786436
  0.7 5.4 %copy-start.4 = (f32[16,16,256]{2,1,0:T(8,128)S(1)}, f32[16,16,256]{2,1,0:T(8,128)}, u32[]{:S(2)}) copy-start(f32[16,16,256]{2,1,0:T(8,128)} %ab.5) | copy-start | bytes 786436
  2.7 9.0 %collective-permute-start = (f32[16,16,256]{2,1,0:T(8,128)}, f32[16,16,256]{2,1,0:T(8,128)S(1)}, u32[]{:S(2)}, u32[]{:S(2)}) collective-permute-start(f32[16,16,256]{2,1,0:T(8,128)} %get-tuple-element.38), channel_id=1, source_target_pairs={{0,16},{16,0},{32,48},{48,32},{64,80},{80,64},{96,112},{112,96},{1... | collective-permute-start | bytes 786440 | tf_op jit(solution)/shard_map/ppermute | solution.py:629
  6.0 6.3 %collective-permute-start.1 = (f32[16,16,256]{2,1,0:T(8,128)}, f32[16,16,256]{2,1,0:T(8,128)S(1)}, u32[]{:S(2)}, u32[]{:S(2)}) collective-permute-start(f32[16,16,256]{2,1,0:T(8,128)} %get-tuple-element.39), channel_id=1, source_target_pairs={{0,240},{16,32},{32,16},{48,64},{64,48},{80,96},{96,80},{112,128},... | collective-permute-start | bytes 786440 | tf_op jit(solution)/shard_map/ppermute | solution.py:629
  6.3 10.6 %collective-permute-start.4 = (f32[8,24,256]{2,1,0:T(8,128)S(1)}, f32[8,24,256]{2,1,0:T(8,128)S(1)}, u32[]{:S(2)}, u32[]{:S(2)}) collective-permute-start(f32[8,24,256]{2,1,0:T(8,128)S(1)} %get-tuple-element.46), channel_id=1, source_target_pairs={{0,1},{1,0},{2,3},{3,2},{4,5},{5,4},{6,7},{7,6},{8,9},{9,8},{10,11... | collective-permute-start | bytes 589832 | tf_op jit(solution)/shard_map/ppermute | solution.py:629
  7.5 9.5 %collective-permute-start.5 = (f32[8,24,256]{2,1,0:T(8,128)S(1)}, f32[8,24,256]{2,1,0:T(8,128)S(1)}, u32[]{:S(2)}, u32[]{:S(2)}) collective-permute-start(f32[8,24,256]{2,1,0:T(8,128)S(1)} %get-tuple-element.47), channel_id=1, source_target_pairs={{0,15},{1,2},{2,1},{3,4},{4,3},{5,6},{6,5},{7,8},{8,7},{9,10},{10,... | collective-permute-start | bytes 589832 | tf_op jit(solution)/shard_map/ppermute | solution.py:629
  12.5 3.5 %copy-start.5 = (s32[1,1,16]{2,1,0:T(1,128)S(1)}, s32[1,1,16]{2,1,0:T(1,128)}, u32[]{:S(2)}) copy-start(s32[1,1,16]{2,1,0:T(1,128)} %active.1) | copy-start | bytes 196
  12.5 5.7 %collective-permute-start.2 = (f32[3,24,256]{2,1,0:T(8,128)S(1)}, f32[3,24,256]{2,1,0:T(8,128)S(1)}, u32[]{:S(2)}, u32[]{:S(2)}) collective-permute-start(f32[3,24,256]{2,1,0:T(8,128)S(1)} %get-tuple-element.41), channel_id=1, source_target_pairs={{0,1},{1,0},{2,3},{3,2},{4,5},{5,4},{6,7},{7,6},{8,9},{9,8},{10,11... | collective-permute-start | bytes 221192 | tf_op jit(solution)/shard_map/ppermute | solution.py:629
  12.6 7.7 %collective-permute-start.3 = (f32[3,24,256]{2,1,0:T(8,128)S(1)}, f32[3,24,256]{2,1,0:T(8,128)S(1)}, u32[]{:S(2)}, u32[]{:S(2)}) collective-permute-start(f32[3,24,256]{2,1,0:T(8,128)S(1)} %get-tuple-element.42), channel_id=1, source_target_pairs={{0,15},{1,2},{2,1},{3,4},{4,3},{5,6},{6,5},{7,8},{8,7},{9,10},{10,... | collective-permute-start | bytes 221192 | tf_op jit(solution)/shard_map/ppermute | solution.py:629
  21.2 8.2 %collective-permute-start.6 = (f32[12,8,128]{2,1,0:T(8,128)S(1)}, f32[12,8,128]{2,1,0:T(8,128)S(1)}, u32[]{:S(2)}, u32[]{:S(2)}) collective-permute-start(f32[12,8,128]{2,1,0:T(8,128)S(1)} %get-tuple-element.58), channel_id=1, source_target_pairs={{0,16},{16,0},{32,48},{48,32},{64,80},{80,64},{96,112},{112,96},{1... | collective-permute-start | bytes 147464 | tf_op jit(solution)/shard_map/ppermute | solution.py:629
  25.7 3.7 %collective-permute-start.7 = (f32[12,8,128]{2,1,0:T(8,128)S(1)}, f32[12,8,128]{2,1,0:T(8,128)S(1)}, u32[]{:S(2)}, u32[]{:S(2)}) collective-permute-start(f32[12,8,128]{2,1,0:T(8,128)S(1)} %get-tuple-element.59), channel_id=1, source_target_pairs={{0,240},{16,32},{32,16},{48,64},{64,48},{80,96},{96,80},{112,128},... | collective-permute-start | bytes 147464 | tf_op jit(solution)/shard_map/ppermute | solution.py:629
  25.7 7.2 %collective-permute-start.8 = (f32[13,8,128]{2,1,0:T(8,128)S(1)}, f32[13,8,128]{2,1,0:T(8,128)S(1)}, u32[]{:S(2)}, u32[]{:S(2)}) collective-permute-start(f32[13,8,128]{2,1,0:T(8,128)S(1)} %get-tuple-element.61), channel_id=1, source_target_pairs={{0,1},{1,0},{2,3},{3,2},{4,5},{5,4},{6,7},{7,6},{8,9},{9,8},{10,11... | collective-permute-start | bytes 159752 | tf_op jit(solution)/shard_map/ppermute | solution.py:629
  25.8 7.1 %collective-permute-start.9 = (f32[13,8,128]{2,1,0:T(8,128)S(1)}, f32[13,8,128]{2,1,0:T(8,128)S(1)}, u32[]{:S(2)}, u32[]{:S(2)}) collective-permute-start(f32[13,8,128]{2,1,0:T(8,128)S(1)} %get-tuple-element.62), channel_id=1, source_target_pairs={{0,15},{1,2},{2,1},{3,4},{4,3},{5,6},{6,5},{7,8},{8,7},{9,10},{10,... | collective-permute-start | bytes 159752 | tf_op jit(solution)/shard_map/ppermute | solution.py:629
  29.5 3.5 %collective-permute-start.10 = (f32[10,8,128]{2,1,0:T(8,128)S(1)}, f32[10,8,128]{2,1,0:T(8,128)S(1)}, u32[]{:S(2)}, u32[]{:S(2)}) collective-permute-start(f32[10,8,128]{2,1,0:T(8,128)S(1)} %get-tuple-element.63), channel_id=1, source_target_pairs={{0,1},{1,0},{2,3},{3,2},{4,5},{5,4},{6,7},{7,6},{8,9},{9,8},{10,11... | collective-permute-start | bytes 122888 | tf_op jit(solution)/shard_map/ppermute | solution.py:629
  29.6 6.3 %collective-permute-start.11 = (f32[10,8,128]{2,1,0:T(8,128)S(1)}, f32[10,8,128]{2,1,0:T(8,128)S(1)}, u32[]{:S(2)}, u32[]{:S(2)}) collective-permute-start(f32[10,8,128]{2,1,0:T(8,128)S(1)} %get-tuple-element.64), channel_id=1, source_target_pairs={{0,15},{1,2},{2,1},{3,4},{4,3},{5,6},{6,5},{7,8},{8,7},{9,10},{10,... | collective-permute-start | bytes 122888 | tf_op jit(solution)/shard_map/ppermute | solution.py:629
